TPU v7x, 32 devices: a whole 2x2x4 slice. The times are simulated.
32 devices in a mesh: fsdp: 32 (over z, y, x, core).
Axes of the slice: x: 2, y: 2, z: 4, core: 2. Of those that a mesh axis runs over, the one named last changes fastest.
Arguments:
- patches: bfloat16 [2, 16384, 768], P(None, 'fsdp'), may hold values from -6 to 6
- tile_kind: int32 [64], P('fsdp'), may hold values from 0 to 2
- out_grad: bfloat16 [2, 16384, 768], P(None, 'fsdp'), may hold values from -6 to 6
- norm1_gain: bfloat16 [2, 768], P(None, 'fsdp'), may hold values from 0.25 to 1.75
- norm1_bias: bfloat16 [2, 768], P(None, 'fsdp'), may hold values from -1.75 to 1.75
- w_qkv: bfloat16 [2, 768, 2304], P(None, 'fsdp'), may hold values from -0.21875 to 0.21875
- w_proj: bfloat16 [2, 768, 768], P(None, 'fsdp'), may hold values from -1.25 to 1.25
- b_proj: bfloat16 [2, 768], P(None, 'fsdp'), may hold values from -3 to 3
- norm2_gain: bfloat16 [2, 768], P(None, 'fsdp'), may hold values from 0.25 to 1.75
- norm2_bias: bfloat16 [2, 768], P(None, 'fsdp'), may hold values from -1.75 to 1.75
- w_fc1: bfloat16 [2, 768, 3072], P(None, 'fsdp'), may hold values from -0.21875 to 0.21875
- b_fc1: bfloat16 [2, 3072], P(None, 'fsdp'), may hold values from -3 to 3
- w_fc2: bfloat16 [2, 3072, 768], P(None, 'fsdp'), may hold values from -0.109375 to 0.109375
- b_fc2: bfloat16 [2, 768], P(None, 'fsdp'), may hold values from -3 to 3
Outputs:
- encoded: bfloat16 [2, 16384, 768], P(None, 'fsdp')
- patches_grad: float32 [2, 16384, 768], P(None, 'fsdp')
- norm1_gain_grad: float32 [2, 768], P(None, 'fsdp')
- norm1_bias_grad: float32 [2, 768], P(None, 'fsdp')
- w_qkv_grad: float32 [2, 768, 2304], P(None, 'fsdp')
- w_proj_grad: float32 [2, 768, 768], P(None, 'fsdp')
- b_proj_grad: float32 [2, 768], P(None, 'fsdp')
- norm2_gain_grad: float32 [2, 768], P(None, 'fsdp')
- norm2_bias_grad: float32 [2, 768], P(None, 'fsdp')
- w_fc1_grad: float32 [2, 768, 3072], P(None, 'fsdp')
- b_fc1_grad: float32 [2, 3072], P(None, 'fsdp')
- w_fc2_grad: float32 [2, 3072, 768], P(None, 'fsdp')
- b_fc2_grad: float32 [2, 768], P(None, 'fsdp')
All inputs are finite; a program needn't handle non-finite values.
Results may differ from a plain program's by a relative error of at most 0.011.
Values may be sent and summed in bfloat16 or wider, within the bound.
A program may use at most 256 MiB of HBM per device.

v0:
```python
import functools

import jax
import jax.numpy as jnp
from jax import lax
from jax.experimental import pallas as pl
from jax.experimental.pallas import tpu as pltpu
from jax.sharding import PartitionSpec as P

HEADS = 12
SIDE_S = 12
SIDE_M = 15
SIDE_L = 20
RING = 32
MESH = pl.DeviceIdType.MESH
BF = jnp.bfloat16
F32 = jnp.float32
FAR = 1e33


def packing(kind_ids, row_count):
    slot_count = kind_ids.shape[0]
    sides = jnp.where(kind_ids == 0, SIDE_S, jnp.where(kind_ids == 1, SIDE_M, SIDE_L)).astype(
        jnp.int32
    )
    lengths = sides * sides
    slots = jnp.arange(slot_count, dtype=jnp.int32)
    ends = jnp.sum(jnp.where(slots[None, :] <= slots[:, None], lengths[None, :], 0), axis=1)
    starts = ends - lengths
    places = jnp.arange(row_count, dtype=jnp.int32)
    inside = (
        (ends <= row_count)[None, :]
        & (places[:, None] >= starts[None, :])
        & (places[:, None] < ends[None, :])
    ).astype(jnp.int32)
    filled = jnp.sum(inside, axis=1)
    segment = jnp.sum(inside * slots[None, :], axis=1) + (1 - filled) * (slot_count + places)
    offset = places - jnp.sum(inside * starts[None, :], axis=1)
    side = jnp.sum(inside * sides[None, :], axis=1) + (1 - filled)
    return segment, offset // side, offset % side, filled


class Place:
    def __init__(self, spread):
        me = lax.axis_index("fsdp")
        rest = lax.rem(me, spread)
        p = me // spread
        self.p = p
        self.c = lax.rem(p, 2)
        self.x = lax.rem(p // 2, 2)
        self.y = lax.rem(p // 4, 2)
        self.m = lax.rem(p // 8, 2)
        self.z = lax.rem(p // 16, 2)
        dev = lambda q: (q * spread + rest,)
        sib = p + 1 - 2 * self.c
        pair = p + 8 * (1 - 2 * self.m)
        self.sib = dev(sib)
        self.xn = dev(p + 2 * (1 - 2 * self.x))
        self.yn = dev(p + 4 * (1 - 2 * self.y))
        self.zn = dev(p + 16 * (1 - 2 * self.z))
        self.pair = dev(pair)
        self.cross = dev(pair + 1 - 2 * self.c)

    def chip(self, fz, fc, fy, fx):
        flip = lambda v, f: 1 - v if f else v
        return (
            (flip(self.z, fz) * 2 + flip(self.c, fc)) * 2 + flip(self.y, fy)
        ) * 2 + flip(self.x, fx)

    def greet(self):
        barrier = pltpu.get_barrier_semaphore()
        everyone = (self.sib, self.xn, self.yn, self.zn, self.pair, self.cross)
        for other in everyone:
            pl.semaphore_signal(barrier, inc=1, device_id=other, device_id_type=MESH)
        pl.semaphore_wait(barrier, len(everyone))


OWN, ZB, X0, X1, Y0, Y1, D0, D1 = range(8)
FLIPS = ((0, 0, 0), (1, 0, 0), (0, 0, 1), (1, 0, 1), (0, 1, 0), (1, 1, 0), (0, 1, 1), (1, 1, 1))


def rcopy(src, dst, ssem, rsem, dev):
    return pltpu.make_async_remote_copy(
        src_ref=src, dst_ref=dst, send_sem=ssem, recv_sem=rsem, device_id=dev, device_id_type=MESH
    )


class Gather:
    def __init__(self, place, full, rows, ssem, rsem):
        self.pl, self.full, self.rows, self.ssem, self.rsem = place, full, rows, ssem, rsem

    def block(self, kind, other=0):
        fz, fy, fx = FLIPS[kind]
        start = self.pl.chip(fz, other, fy, fx) * self.rows
        return self.full.at[pl.ds(pl.multiple_of(start, self.rows), self.rows)]

    def send(self, kind, way):
        place = self.pl
        if way == "s":
            dev, slot = place.sib, 8 + kind
        else:
            dev = {"x": place.xn, "y": place.yn, "z": place.zn}[way]
            fz, fy, fx = FLIPS[kind]
            flips = {"x": (fz, fy, 1 - fx), "y": (fz, 1 - fy, fx), "z": (1 - fz, fy, fx)}[way]
            slot = FLIPS.index(flips)
        view = self.block(kind)
        return rcopy(view, view, self.ssem.at[slot], self.rsem.at[slot], dev)

    AFTER = {
        OWN: "zxys",
        ZB: "xys",
        X0: "ys",
        X1: "s",
        Y0: "s",
        Y1: "xs",
        D0: "s",
        D1: "s",
    }

    def start(self, kind):
        for way in self.AFTER[kind]:
            self.send(kind, way).start()

    def arrived(self, kind, other=0):
        view = self.block(kind, other)
        slot = kind + 8 * other
        rcopy(view, view, self.ssem.at[slot], self.rsem.at[slot], self.pl.sib).wait_recv()

    def finish(self):
        for kind in range(8):
            for way in self.AFTER[kind]:
                self.send(kind, way).wait_send()


def hand_in(place, shard, spot, c_rows, ssem, rsem, go):
    mine, theirs = shard.at[place.m], shard.at[1 - place.m]
    here = lambda: pltpu.make_async_copy(mine, spot(place.c), rsem.at[place.c])
    to_sib = lambda: rcopy(mine, spot(place.c), ssem.at[0], rsem.at[place.c], place.sib)
    to_pair = lambda: rcopy(theirs, spot(place.c), ssem.at[1], rsem.at[place.c], place.pair)
    to_cross = lambda: rcopy(theirs, spot(place.c), ssem.at[1], rsem.at[place.c], place.cross)
    if go == "start":

        @pl.when(place.c == place.m)
        def _():
            here().start()
            to_pair().start()

        @pl.when(place.c != place.m)
        def _():
            to_sib().start()
            to_cross().start()

    elif go == "recv":
        for piece in range(2):
            dst = spot(piece)
            rcopy(dst, dst, ssem.at[1], rsem.at[piece], place.sib).wait_recv()
    else:

        @pl.when(place.c != place.m)
        def _():
            to_sib().wait_send()

        to_pair().wait_send()


def dot(a, b, ca, cb):
    return lax.dot_general(a, b, (((ca,), (cb,)), ((), ())), preferred_element_type=F32)


def chunks(count, step, body):
    @pl.loop(0, count // step)
    def _(i):
        body(pl.ds(pl.multiple_of(i * step, step), step))


def norm(v):
    center = v - jnp.mean(v, axis=-1, keepdims=True)
    r = lax.rsqrt(jnp.mean(center * center, axis=-1, keepdims=True) + 1e-06)
    return center * r, r


def fill_distance(dist, lay):
    across = lay[...]
    down = across.T
    gap_r = down[:, 1:2] - across[1:2]
    gap_c = down[:, 2:3] - across[2:3]
    far = jnp.sqrt(gap_r * gap_r + gap_c * gap_c)
    dist[...] = jnp.where(down[:, 0:1] == across[0:1], far, FAR)


def lanes(half):
    return lax.broadcasted_iota(jnp.int32, (1, 128), 1) // 64 == half


def slope_of(head):
    return jnp.exp2(jnp.full((1, 1), -8.0 / HEADS, F32) * (head + 1).astype(F32))


def attend_pair(qkv, rows, dist, j, prob, slot, o, d):
    col = pl.multiple_of(j * 128, 128)
    q = qkv[rows, pl.ds(col, 128)] * jnp.asarray(0.125, BF)
    k = qkv[rows, pl.ds(d + col, 128)]
    v = qkv[rows, pl.ds(2 * d + col, 128)]
    zero = jnp.zeros((), BF)
    total = None
    for half in range(2):
        keep = lanes(half)
        s = dot(k, jnp.where(keep, q, zero), 1, 1) - slope_of(2 * j + half) * dist
        e = jnp.exp(s - jnp.max(s, axis=0, keepdims=True))
        p = (e * (1.0 / jnp.sum(e, axis=0, keepdims=True))).astype(BF)
        prob[slot + half] = p
        part = dot(jnp.where(keep, v, zero), p, 0, 0)
        total = part if total is None else total + part
    o[rows, pl.ds(col, 128)] = total.T.astype(BF)


def forward_kernel(spread, *refs):
    (pat, dog, lay, wq, wp, w1, w2, sm) = refs[:8]
    (x_o, dog_o, lay_o, wq_o, wp_o, w1_o, w2_o, vec_o, b1_o) = refs[8:17]
    (qkv_o, p_o, o_o, y1_o, c_o, g_o, gs_o, enc_o) = refs[17:25]
    (fq, fp, f1, f2, fs, gq, gp, g1) = refs[25:33]
    (lays, dist, xb, ac, qkv, prob, ob, y1, g, gs) = refs[33:43]
    (hs, hr, ss, rs, as_, ar, ls, ps) = refs[43:]
    place = Place(spread)
    d = xb.shape[2]
    n = xb.shape[1]
    place.greet()
    hand = ((sm, fs, None, 16), (wq, fq, gq, 24), (wp, fp, gp, 24), (w1, f1, g1, 24))
    hand += ((w2, f2, None, w2.shape[1]),)
    gathers = [
        Gather(place, full, 2 * rows, ss.at[k], rs.at[k])
        for k, (_, full, _, rows) in enumerate(hand)
    ]

    def spot_of(k):
        _, full, stage, rows = hand[k]
        if stage is not None:
            return lambda piece: stage.at[piece]
        own = place.chip(0, 0, 0, 0) * 2

        def spot(piece):
            place_of = place.p if piece is place.c else own + piece
            return full.at[pl.ds(pl.multiple_of(place_of * rows, 16), rows)]

        return spot

    def hand_over(k, go):
        hand_in(place, hand[k][0], spot_of(k), hand[k][3], hs.at[k], hr.at[k], go)

    def own_ready(k):
        hand_over(k, "recv")
        _, full, stage, rows = hand[k]
        if stage is not None:
            both = jnp.concatenate([stage[0].astype(F32), stage[1].astype(F32)], axis=0)
            start = pl.multiple_of(place.chip(0, 0, 0, 0) * (2 * rows), 2 * rows)
            full[pl.ds(start, 2 * rows), :] = both.astype(BF)
        gathers[k].start(OWN)

    def pump(k, *kinds):
        for kind in kinds:
            gathers[k].arrived(kind)
            gathers[k].start(kind)

    def whole(k):
        for kind in range(8):
            gathers[k].arrived(kind, 1)

    saves = []

    def save(src, dst):
        copy = pltpu.make_async_copy(src, dst, ls.at[len(saves)])
        copy.start()
        saves.append(copy)

    acts = [
        rcopy(pat.at[1 - place.m], xb.at[1], as_.at[0], ar.at[0], place.pair),
        rcopy(lay, lays.at[1], as_.at[2], ar.at[2], place.pair),
        rcopy(dog.at[1 - place.m], dog_o, as_.at[1], ar.at[1], place.pair),
    ]
    own_x = pltpu.make_async_copy(pat.at[place.m], xb.at[0], ps.at[0])
    own_lay = pltpu.make_async_copy(lay, lays.at[0], ps.at[1])
    for k in range(3):
        hand_over(k, "start")
    own_lay.start()
    own_x.start()
    own_lay.wait()
    fill_distance(dist.at[0], lays.at[0])
    for k in range(3):
        own_ready(k)
    hand_over(3, "start")
    acts[1].start()
    acts[0].start()
    hand_over(4, "start")
    pump(0, ZB, X0, Y0, X1, Y1, D0, D1)
    own_ready(3)
    pump(1, ZB, X0, Y0, X1, Y1, D0, D1)
    own_ready(4)
    acts[2].start()
    whole(0)
    seg = d // RING
    hid = w2.shape[1]
    for q in range(RING):
        tile = fs[16 * q : 16 * q + 16].astype(F32)
        vec_o[0:8, seg * q : seg * q + seg] = tile[0:8, 0:seg]
        b1_o[0:1, hid * q : hid * q + hid] = tile[6:7, 0:hid]
    own_x.wait()

    def first_norm(grp):
        def body(rows):
            nhat, _ = norm(xb[grp, rows, :].astype(F32))
            here = pl.ds(pl.multiple_of(grp * n + rows.start, 128), 128)
            ac[here, :] = (nhat * vec_o[0:1] + vec_o[1:2]).astype(BF)

        chunks(n, 128, body)

    first_norm(0)
    whole(1)
    save(fq, wq_o)
    qkv[0:n] = dot(ac[0:n], fq[...], 1, 0).astype(BF)
    acts[1].wait_recv()
    fill_distance(dist.at[1], lays.at[1])
    acts[0].wait_recv()
    first_norm(1)
    qkv[n : 2 * n] = dot(ac[n : 2 * n], fq[...], 1, 0).astype(BF)
    save(qkv, qkv_o)
    save(xb.at[1], x_o)
    save(lays.at[1], lay_o)
    pairs = HEADS // 2
    early = {
        0: [(2, ZB, X0, Y0)],
        1: [(2, X1, Y1)],
        2: [(2, D0, D1)],
        3: [(3, ZB, X0, Y0)],
        5: [(3, X1, Y1)],
        7: [(3, D0, D1)],
        9: [(4, X0, Y0)],
        10: [(4, ZB)],
    }

    @pl.loop(0, 2 * pairs)
    def _(i):
        grp, j = i // pairs, lax.rem(i, pairs)
        rows = pl.ds(pl.multiple_of(grp * n, n), n)
        attend_pair(qkv, rows, dist[grp], j, prob, 2 * i, ob, d)
        pltpu.make_async_copy(
            prob.at[pl.ds(2 * i, 2)], p_o.at[pl.ds(2 * i, 2)], ps.at[2 + i]
        ).start()
        for at, steps in early.items():

            @pl.when(i == at)
            def _(steps=steps):
                for step in steps:
                    pump(*step)

    save(ob, o_o)
    whole(2)
    save(fp, wp_o)

    def second_norm(rows):
        first = (
            xb[rows.start // n, pl.ds(pl.multiple_of(lax.rem(rows.start, n), 256), 256), :].astype(F32)
            + dot(ob[rows, :], fp[...], 1, 0)
            + vec_o[2:3]
        )
        y1[rows, :] = first
        nhat, _ = norm(first)
        ac[rows, :] = (nhat * vec_o[3:4] + vec_o[4:5]).astype(BF)

    chunks(2 * n, 256, second_norm)
    save(y1, y1_o)
    save(ac, c_o)
    pump(4, X1, Y1)
    whole(3)
    save(f1, w1_o)

    def hidden(cols):
        u = dot(ac[...], f1[:, cols], 1, 0) + b1_o[0:1, cols]
        phi = 0.5 + 0.5 * lax.erf(u * 0.7071067811865476)
        g[:, cols] = (u * phi).astype(BF)
        gs[:, cols] = (phi + u * (0.3989422804014327 * jnp.exp(-0.5 * u * u))).astype(BF)

    chunks(g.shape[1], 256, hidden)
    save(g, g_o)
    save(gs, gs_o)
    pump(4, D0, D1)
    whole(4)
    save(f2, w2_o)

    def result(rows):
        ac_rows = y1[rows, :] + dot(g[rows, :], f2[...], 1, 0) + vec_o[5:6]
        qkv[rows, 0:d] = ac_rows.astype(BF)

    saves[1].wait()
    chunks(2 * n, 512, result)
    save(qkv.at[:, pl.ds(0, d)], enc_o)
    for k in range(5):
        hand_over(k, "send")
        gathers[k].finish()
    acts[0].wait_send()
    acts[1].wait_send()
    acts[2].wait()
    for i in range(2 * pairs):
        pltpu.make_async_copy(
            prob.at[pl.ds(2 * i, 2)], p_o.at[pl.ds(2 * i, 2)], ps.at[2 + i]
        ).wait()
    for k, copy in enumerate(saves):
        if k != 1:
            copy.wait()


def forward(spread, pat, dog, lay, wq, wp, w1, w2, sm):
    any_, vm = pl.BlockSpec(memory_space=pl.ANY), pl.BlockSpec(memory_space=pltpu.VMEM)
    n, d = pat.shape[1:]
    ff = w2.shape[1] * RING
    sd = jax.ShapeDtypeStruct
    out = [
        sd((n, d), BF),
        sd((n, d), BF),
        sd(lay.shape, F32),
        sd((d, wq.shape[2]), BF),
        sd((d, d), BF),
        sd((d, ff), BF),
        sd((ff, d), BF),
        sd((8, d), F32),
        sd((8, ff), F32),
        sd((2 * n, wq.shape[2]), BF),
        sd((2 * HEADS, n, n), BF),
        sd((2 * n, d), BF),
        sd((2 * n, d), F32),
        sd((2 * n, d), BF),
        sd((2 * n, ff), BF),
        sd((2 * n, ff), BF),
        sd((2 * n, d), BF),
    ]
    dma = pltpu.SemaphoreType.DMA
    vmem = pltpu.VMEM
    return pl.pallas_call(
        functools.partial(forward_kernel, spread),
        out_shape=out,
        in_specs=[any_] * 8,
        out_specs=[any_] * 7 + [vm] * 2 + [any_] * 8,
        scratch_shapes=[
            vmem((d, wq.shape[2]), BF),
            vmem((d, d), BF),
            vmem((d, ff), BF),
            vmem((ff, d), BF),
            vmem((RING * 16, 128), BF),
            vmem((2, 24, wq.shape[2]), BF),
            vmem((2, 24, d), BF),
            vmem((2, 24, ff), BF),
            vmem((2,) + lay.shape, F32),
            vmem((2, n, n), F32),
            vmem((2, n, d), BF),
            vmem((2 * n, d), BF),
            vmem((2 * n, wq.shape[2]), BF),
            vmem((2 * HEADS, n, n), BF),
            vmem((2 * n, d), BF),
            vmem((2 * n, d), F32),
            vmem((2 * n, ff), BF),
            vmem((2 * n, ff), BF),
            dma((5, 2)),
            dma((5, 2)),
            dma((5, 16)),
            dma((5, 16)),
            dma((3,)),
            dma((3,)),
            dma((16,)),
            dma((2 + HEADS,)),
        ],
        compiler_params=pltpu.CompilerParams(
            collective_id=0, has_side_effects=True, vmem_limit_bytes=62 * 2**20
        ),
        name="forward",
    )(pat, dog, lay, wq, wp, w1, w2, sm)


class Scatter:
    def __init__(self, place, full, rows, got_sib, got, ssem, rsem):
        self.pl, self.full, self.rows = place, full, rows
        self.got_sib, self.got, self.ssem, self.rsem = got_sib, got, ssem, rsem

    def start_of(self, kind):
        fz, fy, fx = FLIPS[kind]
        return pl.multiple_of(self.pl.chip(fz, 0, fy, fx) * self.rows, self.rows)

    def plane(self, z, other):
        c = 1 - self.pl.c if other else self.pl.c
        return pl.ds(pl.multiple_of((z * 2 + c) * (4 * self.rows), self.rows), 4 * self.rows)

    def sib(self, z):
        return rcopy(
            self.full.at[self.plane(z, 1)],
            self.got_sib.at[z],
            self.ssem.at[z],
            self.rsem.at[z],
            self.pl.sib,
        )

    MOVES = {D0: ("y", 0), D1: ("x", 1), X0: ("x", 2), X1: ("x", 3), Y0: ("y", 4), Y1: ("y", 5), ZB: ("z", 6)}

    def move(self, kind):
        way, slot = self.MOVES[kind]
        dev = {"x": self.pl.xn, "y": self.pl.yn, "z": self.pl.zn}[way]
        return rcopy(
            self.full.at[pl.ds(self.start_of(kind), self.rows)],
            self.got.at[slot],
            self.ssem.at[2 + slot],
            self.rsem.at[2 + slot],
            dev,
        )

    def add(self, kind, slots):
        rows = pl.ds(self.start_of(kind), self.rows)
        total = self.full[rows, :].astype(F32)
        for slot in slots:
            total = total + self.got[slot].astype(F32)
        self.full[rows, :] = total.astype(BF)

    def begin(self):
        self.sib(0).start()
        self.sib(1).start()

    def second(self):
        for z in range(2):
            self.sib(z).wait()
        step = 16

        for z in range(2):
            base = (z * 2 + self.pl.c) * (4 * self.rows)

            @pl.loop(0, 4 * self.rows // step)
            def _(i, z=z, base=base):
                rows = pl.ds(pl.multiple_of(base + i * step, step), step)
                theirs = self.got_sib[z, pl.ds(pl.multiple_of(i * step, step), step), :]
                self.full[rows, :] = (self.full[rows, :].astype(F32) + theirs.astype(F32)).astype(BF)

        for kind in (D0, D1, X1, Y0):
            self.move(kind).start()

    def third(self):
        self.move(D0).wait()
        self.add(X0, (0,))
        self.move(X0).start()
        self.move(D1).wait()
        self.add(Y1, (1,))
        self.move(Y1).start()

    def fourth(self):
        self.move(X1).wait()
        self.move(Y1).wait()
        self.add(ZB, (3, 5))
        self.move(ZB).start()

    def total(self):
        self.move(X0).wait()
        self.move(Y0).wait()
        self.move(ZB).wait()
        rows = pl.ds(self.start_of(OWN), self.rows)
        total = self.full[rows, :].astype(F32)
        for slot in (2, 4, 6):
            total = total + self.got[slot].astype(F32)
        return total


def hand_back(place, stage, out, ssem, rsem, go):
    if go == "start":

        @pl.when(place.c == place.m)
        def _():
            pltpu.make_async_copy(stage.at[place.c], out.at[place.m], rsem.at[place.m]).start()
            rcopy(
                stage.at[1 - place.c], out.at[place.m], ssem.at[0], rsem.at[place.m], place.sib
            ).start()

        @pl.when(place.c != place.m)
        def _():
            rcopy(
                stage.at[place.c], out.at[place.m], ssem.at[0], rsem.at[place.m], place.pair
            ).start()
            rcopy(
                stage.at[1 - place.c], out.at[place.m], ssem.at[1], rsem.at[place.m], place.cross
            ).start()

    elif go == "recv":
        for k in range(2):
            rcopy(out.at[k], out.at[k], ssem.at[0], rsem.at[k], place.sib).wait_recv()
    else:
        rcopy(stage.at[0], out.at[0], ssem.at[0], rsem.at[0], place.sib).wait_send()

        @pl.when(place.c != place.m)
        def _():
            rcopy(stage.at[0], out.at[0], ssem.at[1], rsem.at[0], place.sib).wait_send()


def unnorm(dn, nhat, r, gain):
    dh = dn * gain
    return r * (
        dh - jnp.mean(dh, axis=-1, keepdims=True) - nhat * jnp.mean(dh * nhat, axis=-1, keepdims=True)
    )


def attend_back(qkv, rows, probs, do, o, j, d):
    col = pl.multiple_of(j * 128, 128)
    eighth = jnp.asarray(0.125, BF)
    zero = jnp.zeros((), BF)
    q = qkv[rows, pl.ds(col, 128)]
    k = qkv[rows, pl.ds(d + col, 128)]
    v = qkv[rows, pl.ds(2 * d + col, 128)]
    g = do[rows, pl.ds(col, 128)]
    both = g.astype(F32) * o[rows, pl.ds(col, 128)].astype(F32)
    dq = dk = dv = 0.0
    for half in range(2):
        keep = lanes(half)
        p = probs[half]
        gm = jnp.where(keep, g, zero)
        centre = jnp.sum(jnp.where(keep, both, 0.0), axis=1, keepdims=True)
        centre = jnp.broadcast_to(centre, (both.shape[0], 128)).T[0:1]
        ds = (p.astype(F32) * (dot(v, gm, 1, 1) - centre)).astype(BF)
        dk = dk + dot(ds, jnp.where(keep, q * eighth, zero), 1, 0)
        dv = dv + dot(p, gm, 1, 0)
        dq = dq + dot(jnp.where(keep, k * eighth, zero), ds, 0, 0)
    qkv[rows, pl.ds(col, 128)] = dq.T.astype(BF)
    qkv[rows, pl.ds(d + col, 128)] = dk.astype(BF)
    qkv[rows, pl.ds(2 * d + col, 128)] = dv.astype(BF)


def backward_kernel(spread, *refs):
    (pat, dog, lay, x_i, dog_i, lay_i, wq_i, wp_i, w1_i, w2_i, vec) = refs[:11]
    (qkv_i, p_i, o_i, y1_i, c_i, g_i, gs_i, y_i) = refs[11:19]
    (oq, op, o1, o2, os_, enc_o, pg_o) = refs[19:26]
    (w2, w1, wp, qkv, g, du, c, ob, dz, y1, do, g2, gp, lays, sums) = refs[26:41]
    got_sib, got, stages = refs[41:45], refs[45:49], refs[49:53]
    (sgot, ss, rs, hs, hr, es, er, ts, tr, ls, ps) = refs[53:]
    place = Place(spread)
    n, d = c.shape[0] // 2, c.shape[1]
    ff = w1.shape[1]
    wide = qkv.shape[1]
    loads = []

    def load(src, dst):
        copy = pltpu.make_async_copy(src, dst, ls.at[len(loads)])
        copy.start()
        loads.append(copy)
        return copy

    lay_l = (load(lay, lays.at[0]), load(lay_i, lays.at[1]))
    dz_l = (
        load(dog.at[place.m], dz.at[pl.ds(0, n)]),
        load(dog_i, dz.at[pl.ds(n, n)]),
    )
    g_l = load(g_i, g)
    w2_l = load(w2_i, w2)
    du_l = load(gs_i, du)
    c_l = load(c_i, c)
    w1_l = load(w1_i, w1)
    y1_l = load(y1_i, y1)
    o_l = load(o_i, ob)
    wp_l = load(wp_i, wp)
    qkv_l = load(qkv_i, qkv)
    place.greet()
    acts = [
        rcopy(y_i.at[pl.ds(n, n)], enc_o.at[place.m], es.at[0], er.at[0], place.pair),
        rcopy(c.at[pl.ds(n, n)], pg_o.at[place.m], es.at[1], er.at[1], place.pair),
    ]
    enc_l = load(y_i.at[pl.ds(0, n)], enc_o.at[place.m])
    acts[0].start()
    gq = du.at[pl.ds(0, d), pl.ds(0, wide)]
    g1 = g.at[pl.ds(0, d)]
    fulls = (gq, gp, g1, g2)
    outs = (oq, op, o1, o2)
    rows_of = (48, 48, 48, ff // 16)
    sc = [
        Scatter(place, fulls[k], rows_of[k], got_sib[k], got[k], ss.at[k], rs.at[k])
        for k in range(4)
    ]

    def close(k):
        total = sc[k].total()
        half = rows_of[k] // 2
        stages[k][0] = total[:half].astype(BF)
        stages[k][1] = total[half:].astype(BF)
        hand_back(place, stages[k], outs[k], hs.at[k], hr.at[k], "start")

    QK, PR, W1, W2 = range(4)
    sums[...] = jnp.zeros_like(sums)

    def add_sum(row, v):
        sums[row : row + 1] += jnp.sum(v, axis=0, keepdims=True)

    for copy in (*lay_l, *dz_l):
        copy.wait()
    for grp in range(2):
        live = lays[grp].T[:, 3:4]

        for part in range(4):
            rows = pl.ds(grp * n + part * (n // 4), n // 4)
            keep = live[part * (n // 4) : (part + 1) * (n // 4)]
            v = dz[rows, :].astype(F32) * keep
            dz[rows, :] = v.astype(BF)
            add_sum(5, v)
    g_l.wait()

    @pl.loop(0, 4)
    def _(i):
        z, other = lax.rem(i, 2), 1 - i // 2
        start = (z * 2 + jnp.where(other == 1, 1 - place.c, place.c)) * (ff // 4)
        cols = pl.ds(pl.multiple_of(start, 128), ff // 4)
        g2[cols, :] = dot(g[:, cols], dz[...], 0, 0).astype(BF)

        @pl.when(i == 1)
        def _():
            sc[W2].begin()

    w2_l.wait()
    du_l.wait()

    def hidden(cols):
        v = dot(dz[...], w2[cols, :], 1, 1) * du[:, cols].astype(F32)
        r = v.astype(BF)
        du[:, cols] = r
        line = jnp.sum(r.astype(F32), axis=0, keepdims=True)
        sums[pl.ds(6 + cols.start // d, 1), pl.ds(pl.multiple_of(lax.rem(cols.start, d), 128), 256)] = line

    chunks(ff, 256, hidden)
    sc[W2].second()
    pairs = HEADS // 2

    def fetch(i):
        src = lax.rem(i + pairs, 2 * pairs) * 2
        slot = lax.rem(i, 3)
        for half in range(2):
            yield pltpu.make_async_copy(
                p_i.at[src + half],
                w2.at[pl.ds(pl.multiple_of((slot * 2 + half) * n, n), n), pl.ds(0, n)],
                ps.at[slot, half],
            )

    for i in range(3):
        for copy in fetch(i):
            copy.start()
    c_l.wait()

    def up_grad(cols):
        g1[:, cols] = dot(c[...], du[:, cols], 0, 0).astype(BF)

    chunks(ff, 768, up_grad)
    sc[W1].begin()
    sc[W2].third()
    w1_l.wait()
    y1_l.wait()

    def second_norm(rows):
        dc = dot(du[rows, :], w1[...], 1, 1)
        nhat, r = norm(y1[rows, :])
        add_sum(3, dc * nhat)
        add_sum(4, dc)
        first = dz[rows, :].astype(F32) + unnorm(dc, nhat, r, vec[3:4])
        y1[rows, :] = first
        low = first.astype(BF)
        c[rows, :] = low
        add_sum(2, low.astype(F32))

    def span(start, count, step, body):
        chunks(count, step, lambda s: body(pl.ds(pl.multiple_of(start + s.start, step), step)))

    span(0, n, 256, second_norm)
    sc[W1].second()
    span(n, n, 256, second_norm)
    wq_l = load(wq_i, w1.at[:, pl.ds(0, wide)])
    sc[W2].fourth()
    o_l.wait()
    wp_l.wait()
    gp[...] = dot(ob[...], c[...], 0, 0).astype(BF)
    sc[PR].begin()
    do[...] = dot(c[...], wp[...], 1, 1).astype(BF)
    x_l = (load(pat.at[place.m], c.at[pl.ds(0, n)]), load(x_i, c.at[pl.ds(n, n)]))
    sc[W1].third()
    for copy in x_l:
        copy.wait()

    def first_norm(rows):
        nhat, _ = norm(c[rows, :].astype(F32))
        dz[rows, :] = (nhat * vec[0:1] + vec[1:2]).astype(BF)

    chunks(2 * n, 256, first_norm)
    qkv_l.wait()
    work = {
        0: lambda: sc[PR].second(),
        1: lambda: close(W2),
        3: lambda: sc[PR].third(),
        4: lambda: sc[W1].fourth(),
        7: lambda: sc[PR].fourth(),
        8: lambda: close(W1),
        10: lambda: close(PR),
    }

    def attention(start):
        @pl.loop(start, start + pairs)
        def _(i):
            j = lax.rem(i, pairs)
            grp = 1 - i // pairs
            rows = pl.ds(pl.multiple_of(grp * n, n), n)
            for copy in fetch(i):
                copy.wait()
            slot = lax.rem(i, 3)
            probs = [
                w2.at[pl.ds(pl.multiple_of((slot * 2 + half) * n, n), n), pl.ds(0, n)]
                for half in range(2)
            ]
            attend_back(qkv, rows, [p[...] for p in probs], do, ob, j, d)

            @pl.when(i + 3 < 2 * pairs)
            def _():
                for copy in fetch(i + 3):
                    copy.start()

            for at, step in work.items():
                if start <= at < start + pairs:

                    @pl.when(i == at)
                    def _(step=step):
                        step()

    def input_grad(rows):
        da = dot(qkv[rows, :], w1[:, pl.ds(0, wide)], 1, 1)
        nhat, r = norm(c[rows, :].astype(F32))
        add_sum(0, da * nhat)
        add_sum(1, da)
        c[rows, :] = (y1[rows, :] + unnorm(da, nhat, r, vec[0:1])).astype(BF)

    attention(0)
    wq_l.wait()
    span(n, n, 256, input_grad)
    acts[1].start()
    attention(pairs)

    def qkv_grad(cols):
        gq[:, cols] = dot(dz[...], qkv[:, cols], 0, 0).astype(BF)

    chunks(wide, 768, qkv_grad)
    sc[QK].begin()
    span(0, n, 256, input_grad)
    pg_l = load(c.at[pl.ds(0, n)], pg_o.at[place.m])
    os_[place.m] = sums[...]
    hops = (place.sib, place.xn, place.yn, place.zn)

    def hop(i):
        return rcopy(os_.at[place.m], sgot.at[i], ts.at[i], tr.at[i], hops[i])

    def landed(i):
        hop(i).wait()
        os_[place.m] = os_[place.m] + sgot[i]

    hop(0).start()
    sc[QK].second()
    landed(0)
    hop(1).start()
    sc[QK].third()
    landed(1)
    hop(2).start()
    sc[QK].fourth()
    landed(2)
    hop(3).start()
    close(QK)
    landed(3)
    last = rcopy(os_.at[place.m], os_.at[place.m], ts.at[4], tr.at[4], place.pair)
    last.start()
    for k in (W2, W1, PR, QK):
        hand_back(place, stages[k], outs[k], hs.at[k], hr.at[k], "recv")
        hand_back(place, stages[k], outs[k], hs.at[k], hr.at[k], "send")
    last.wait_send()
    theirs = os_.at[1 - place.m]
    rcopy(theirs, theirs, ts.at[4], tr.at[4], place.pair).wait_recv()
    for act in acts:
        act.wait()
    enc_l.wait()
    pg_l.wait()


def backward(spread, pat, dog, lay, *kept):
    any_, vm = pl.BlockSpec(memory_space=pl.ANY), pl.BlockSpec(memory_space=pltpu.VMEM)
    n, d = pat.shape[1:]
    wide, ff = kept[3].shape[1], kept[5].shape[1]
    shapes = ((48, wide), (48, d), (48, ff), (ff // 16, d))
    sd = jax.ShapeDtypeStruct
    out = [sd((2, r // 2, k), BF) for r, k in shapes]
    out += [sd((2, 16, d), F32), sd((2, n, d), BF), sd((2, n, d), BF)]
    dma = pltpu.SemaphoreType.DMA
    vmem = pltpu.VMEM
    return pl.pallas_call(
        functools.partial(backward_kernel, spread),
        out_shape=out,
        in_specs=[any_] * 10 + [vm] + [any_] * 8,
        out_specs=[any_] * 4 + [vm] + [any_] * 2,
        scratch_shapes=[
            vmem((ff, d), BF),
            vmem((d, ff), BF),
            vmem((d, d), BF),
            vmem((2 * n, wide), BF),
            vmem((2 * n, ff), BF),
            vmem((2 * n, ff), BF),
            vmem((2 * n, d), BF),
            vmem((2 * n, d), BF),
            vmem((2 * n, d), BF),
            vmem((2 * n, d), F32),
            vmem((2 * n, d), BF),
            vmem((ff, d), BF),
            vmem((d, d), BF),
            vmem((2,) + lay.shape, F32),
            vmem((16, d), F32),
        ]
        + [vmem((2, 4 * r, k), BF) for r, k in shapes]
        + [vmem((7, r, k), BF) for r, k in shapes]
        + [vmem((2, r // 2, k), BF) for r, k in shapes]
        + [
            vmem((4, 16, d), F32),
            dma((4, 9)),
            dma((4, 9)),
            dma((4, 2)),
            dma((4, 2)),
            dma((2,)),
            dma((2,)),
            dma((5,)),
            dma((5,)),
            dma((18,)),
            dma((3, 2)),
        ],
        compiler_params=pltpu.CompilerParams(
            collective_id=1, has_side_effects=True, vmem_limit_bytes=62 * 2**20
        ),
        name="backward",
    )(pat, dog, lay, *kept)


def small_pack(parts, b1):
    rows = jnp.stack([jnp.pad(v, ((0, 0), (0, 128 - v.shape[1]))) for v in (*parts, b1)], axis=1)
    return jnp.pad(rows, ((0, 0), (0, 16 - rows.shape[1]), (0, 0)))


def local(
    count, patches, tile_kind, out_grad, n1g, n1b, wq, wp, bp, n2g, n2b, w1, b1, w2, b2
):
    spread = count // RING
    idx = lax.axis_index("fsdp")
    p = idx // spread
    rows, d = patches.shape[1:]
    parts = (n1g, n1b, bp, n2g, n2b, b2)
    if spread > 1:
        groups = [[q * spread + j for j in range(spread)] for q in range(RING)]
        ag = functools.partial(
            lax.all_gather, axis_name="fsdp", axis=1, tiled=True, axis_index_groups=groups
        )
        wq, wp, w1, w2, b1 = ag(wq), ag(wp), ag(w1), ag(w2), ag(b1)
        parts = tuple(ag(v) for v in parts)
    lay = jnp.stack([v.astype(F32) for v in packing(tile_kind, rows)])
    lay = jnp.pad(lay, ((0, 4), (0, 0)))
    sm = small_pack(parts, b1)
    pat2, dog2, lay2, fq, fp, f1, f2, vecs, _, *saved = forward(
        spread, patches, out_grad, lay, wq, wp, w1, w2, sm
    )
    oq, op, o1, o2, os_, encoded, pgrad = backward(
        spread, patches, out_grad, lay, pat2, dog2, lay2, fq, fp, f1, f2, vecs, *saved
    )
    pgrad = pgrad.astype(F32)
    seg = d // RING
    vec = lax.dynamic_slice_in_dim(os_[:, :6], p * seg, seg, axis=2)
    hid = os_[:, 6 : 6 + w2.shape[1] * RING // d].reshape(2, -1)
    hid = lax.dynamic_slice_in_dim(hid, p * w2.shape[1], w2.shape[1], axis=1)
    grads = [oq.astype(F32), op.astype(F32), o1.astype(F32), o2.astype(F32)]
    if spread > 1:
        rs = functools.partial(
            lax.psum_scatter, axis_name="fsdp", tiled=True, axis_index_groups=groups
        )
        grads = [rs(v, scatter_dimension=1) for v in grads]
        vec, hid = rs(vec, scatter_dimension=2), rs(hid, scatter_dimension=1)
    return (
        encoded,
        pgrad,
        vec[:, 0],
        vec[:, 1],
        grads[0],
        grads[1],
        vec[:, 2],
        vec[:, 3],
        vec[:, 4],
        grads[2],
        hid,
        grads[3],
        vec[:, 5],
    )


def solution(mesh):
    three, two = P(None, "fsdp", None), P(None, "fsdp")
    in_specs = (three, P("fsdp"), three, two, two, three, three, two, two, two, three, two, three, two)
    out_specs = (three, three, two, two, three, three, two, two, two, three, two, three, two)
    return jax.shard_map(
        functools.partial(local, mesh.shape["fsdp"]),
        mesh=mesh,
        in_specs=in_specs,
        out_specs=out_specs,
        check_vma=False,
    )
```

profile of v0, /device:TPU:0, one launch (start us, length us, event | category | flops | bytes accessed | tf_op | source)
XLA Modules:
  0.0 265.0 jit_solution(6717668070684577212)
XLA Ops:
  0.6 0.7 fusion.3
  1.3 0.1 fusion.2
  1.4 0.1 select_reduce_fusion.2
  1.6 0.4 fusion
  1.9 0.6 select_maximum_fusion.refs_2_
  2.6 0.7 pad_bitcast_fusion.6
  3.2 0.7 pad_bitcast_fusion.5
  3.9 0.7 pad_bitcast_fusion.4
  4.6 0.7 pad_bitcast_fusion.3
  5.2 0.7 pad_bitcast_fusion.2
  5.9 0.7 pad_bitcast_fusion.1
  6.6 0.7 pad_bitcast_fusion
  7.3 0.6 pad.39.refs_7_
  7.9 113.4 %forward.1 = (bf16[512,768]{1,0:T(8,128)(2,1)}, bf16[512,768]{1,0:T(8,128)(2,1)}, f32[8,512]{1,0:T(8,128)}, bf16[768,2304]{1,0:T(8,128)(2,1)}, bf16[768,768]{1,0...) custom-call(bf16[2,512,768]{2,1,0:T(8,128)(2,1)} %refs_0_.3, ...), custom_call_target="tpu_custom_call" | custom-call | tf_op jit(solution)/shard_map/forward/pallas_call | solution.py:437
  121.2 134.5 %backward.1 = (bf16[2,24,2304]{2,1,0:T(8,128)(2,1)}, bf16[2,24,768]{2,1,0:T(8,128)(2,1)}, bf16[2,24,3072]{2,1,0:T(8,128)(2,1)}, bf16[2,96,768]{2,1,0:T(8,128)(2,...) custom-call(bf16[2,512,768]{2,1,0:T(8,128)(2,1)} %refs_0_.3, ...), custom_call_target="tpu_custom_call" | custom-call | tf_op jit(solution)/shard_map/backward/pallas_call | solution.py:890
  255.8 0.0 copy-start.2
  255.8 0.0 copy-start.1
  255.8 0.0 copy-start.3
  255.8 0.0 copy-start.4
  255.8 0.0 copy-start.5
  255.9 0.0 copy-start
  255.9 3.5 %convert_element_type.80 = f32[2,512,768]{2,1,0:T(8,128)} convert(bf16[2,512,768]{2,1,0:T(8,128)(2,1)} %get-tuple-element.53) | non-fusion elementwise | flops 786432 | bytes 4718592 | tf_op jit(solution)/shard_map/convert_element_type | solution.py:964
  259.3 0.0 copy-done.2
  259.3 0.9 convert_element_type.83
  260.2 0.9 convert_element_type.84
  261.0 0.0 copy-done.3
  261.0 0.8 convert_element_type.81
  261.8 0.7 convert_element_type.82
  262.5 0.7 constant_dynamic-slice_fusion.6
  263.2 0.6 constant_dynamic-slice_fusion.5
  263.9 0.0 copy-done
  263.9 1.1 copy.43
  (17 shorter events, 0.1 us)
Async XLA Ops:
  255.8 3.5 %copy-start.2 = (bf16[2,24,3072]{2,1,0:T(8,128)(2,1)S(1)}, bf16[2,24,3072]{2,1,0:T(8,128)(2,1)}, u32[]{:S(2)}) copy-start(bf16[2,24,3072]{2,1,0:T(8,128)(2,1)} %get-tuple-element.57) | copy-start | bytes 884740
  255.8 4.4 %copy-start.1 = (bf16[2,96,768]{2,1,0:T(8,128)(2,1)S(1)}, bf16[2,96,768]{2,1,0:T(8,128)(2,1)}, u32[]{:S(2)}) copy-start(bf16[2,96,768]{2,1,0:T(8,128)(2,1)} %get-tuple-element.58) | copy-start | bytes 884740
  255.8 5.2 %copy-start.3 = (bf16[2,24,2304]{2,1,0:T(8,128)(2,1)S(1)}, bf16[2,24,2304]{2,1,0:T(8,128)(2,1)}, u32[]{:S(2)}) copy-start(bf16[2,24,2304]{2,1,0:T(8,128)(2,1)} %get-tuple-element.55) | copy-start | bytes 663556
  255.8 6.0 %copy-start.4 = (bf16[2,24,768]{2,1,0:T(8,128)(2,1)S(1)}, bf16[2,24,768]{2,1,0:T(8,128)(2,1)}, u32[]{:S(2)}) copy-start(bf16[2,24,768]{2,1,0:T(8,128)(2,1)} %get-tuple-element.56) | copy-start | bytes 221188
  255.8 6.7 %copy-start.5 = (f32[2,16,768]{2,1,0:T(8,128)S(1)}, f32[2,16,768]{2,1,0:T(8,128)}, u32[]{:S(2)}) copy-start(f32[2,16,768]{2,1,0:T(8,128)} %get-tuple-element.54) | copy-start | bytes 294916
  255.9 8.0 %copy-start = (bf16[2,512,768]{2,1,0:T(8,128)(2,1)S(1)}, bf16[2,512,768]{2,1,0:T(8,128)(2,1)}, u32[]{:S(2)}) copy-start(bf16[2,512,768]{2,1,0:T(8,128)(2,1)} %get-tuple-element.89) | copy-start | bytes 4718596
where the time goes:
time: 265 us
  Pallas kernels  248 us (94%)
  other arithmetic  8.53 us (3%)
  local copies, waits for them, and re-layouts  7.8 us (3%)
    pallas_call x1, Pallas kernels, backward(): pl.pallas_call(functools.partial(backward_kernel, spread), out_shape=out,...  135 us
    pallas_call x1, Pallas kernels, forward(): pl.pallas_call(functools.partial(forward_kernel, spread), out_shape=out,...  113 us

commit v1 on v0

--- a/solution.py
+++ b/solution.py
@@ -196,11 +196,18 @@
     return jnp.exp2(jnp.full((1, 1), -8.0 / HEADS, F32) * (head + 1).astype(F32))
 
 
+def head_columns(j, d):
+    pairs = HEADS // 4
+    base = (j // pairs) * (3 * d // 2) + lax.rem(j, pairs) * 128
+    return [pl.ds(pl.multiple_of(base + part * (d // 2), 128), 128) for part in range(3)]
+
+
 def attend_pair(qkv, rows, dist, j, prob, slot, o, d):
     col = pl.multiple_of(j * 128, 128)
-    q = qkv[rows, pl.ds(col, 128)] * jnp.asarray(0.125, BF)
-    k = qkv[rows, pl.ds(d + col, 128)]
-    v = qkv[rows, pl.ds(2 * d + col, 128)]
+    cq, ck, cv = head_columns(j, d)
+    q = qkv[rows, cq] * jnp.asarray(0.125, BF)
+    k = qkv[rows, ck]
+    v = qkv[rows, cv]
     zero = jnp.zeros((), BF)
     total = None
     for half in range(2):
@@ -224,12 +231,24 @@
     place = Place(spread)
     d = xb.shape[2]
     n = xb.shape[1]
+    ff = g.shape[1]
     place.greet()
     hand = ((sm, fs, None, 16), (wq, fq, gq, 24), (wp, fp, gp, 24), (w1, f1, g1, 24))
     hand += ((w2, f2, None, w2.shape[1]),)
-    gathers = [
-        Gather(place, full, 2 * rows, ss.at[k], rs.at[k])
-        for k, (_, full, _, rows) in enumerate(hand)
+    SM, QA, QB, PR, UA, UB, DA, DB = range(8)
+    half = 3 * d // 2
+    cut = (
+        (0, fs),
+        (1, fq.at[:, pl.ds(0, half)]),
+        (1, fq.at[:, pl.ds(half, half)]),
+        (2, fp),
+        (3, f1.at[:, pl.ds(0, ff // 2)]),
+        (3, f1.at[:, pl.ds(ff // 2, ff // 2)]),
+        (4, f2.at[:, pl.ds(0, d // 2)]),
+        (4, f2.at[:, pl.ds(d // 2, d // 2)]),
+    )
+    pieces = [
+        Gather(place, view, 2 * hand[k][3], ss.at[i], rs.at[i]) for i, (k, view) in enumerate(cut)
     ]
 
     def spot_of(k):
@@ -251,19 +270,33 @@
         hand_over(k, "recv")
         _, full, stage, rows = hand[k]
         if stage is not None:
-            both = jnp.concatenate([stage[0].astype(F32), stage[1].astype(F32)], axis=0)
             start = pl.multiple_of(place.chip(0, 0, 0, 0) * (2 * rows), 2 * rows)
-            full[pl.ds(start, 2 * rows), :] = both.astype(BF)
-        gathers[k].start(OWN)
-
-    def pump(k, *kinds):
+
+            def pack(src, dst):
+                both = [stage[piece, :, src].astype(F32) for piece in range(2)]
+                full[pl.ds(start, 2 * rows), dst] = jnp.concatenate(both, axis=0).astype(BF)
+
+            if k == 1:
+                for part in range(3):
+                    for side in range(2):
+                        pack(
+                            pl.ds(part * d + side * (d // 2), d // 2),
+                            pl.ds((side * 3 + part) * (d // 2), d // 2),
+                        )
+            else:
+                pack(pl.ds(0, full.shape[1]), pl.ds(0, full.shape[1]))
+        for i, (at, _) in enumerate(cut):
+            if at == k:
+                pieces[i].start(OWN)
+
+    def pump(i, *kinds):
         for kind in kinds:
-            gathers[k].arrived(kind)
-            gathers[k].start(kind)
-
-    def whole(k):
+            pieces[i].arrived(kind)
+            pieces[i].start(kind)
+
+    def whole(i):
         for kind in range(8):
-            gathers[k].arrived(kind, 1)
+            pieces[i].arrived(kind, 1)
 
     saves = []
 
@@ -271,39 +304,27 @@
         copy = pltpu.make_async_copy(src, dst, ls.at[len(saves)])
         copy.start()
         saves.append(copy)
-
-    acts = [
-        rcopy(pat.at[1 - place.m], xb.at[1], as_.at[0], ar.at[0], place.pair),
-        rcopy(lay, lays.at[1], as_.at[2], ar.at[2], place.pair),
-        rcopy(dog.at[1 - place.m], dog_o, as_.at[1], ar.at[1], place.pair),
-    ]
+        return copy
+
+    send_x = rcopy(pat.at[1 - place.m], xb.at[1], as_.at[0], ar.at[0], place.pair)
+    send_dog = rcopy(dog.at[1 - place.m], dog_o, as_.at[1], ar.at[1], place.pair)
+    send_lay = rcopy(lay, lays.at[1], as_.at[2], ar.at[2], place.pair)
     own_x = pltpu.make_async_copy(pat.at[place.m], xb.at[0], ps.at[0])
     own_lay = pltpu.make_async_copy(lay, lays.at[0], ps.at[1])
-    for k in range(3):
-        hand_over(k, "start")
     own_lay.start()
     own_x.start()
-    own_lay.wait()
-    fill_distance(dist.at[0], lays.at[0])
-    for k in range(3):
-        own_ready(k)
-    hand_over(3, "start")
-    acts[1].start()
-    acts[0].start()
-    hand_over(4, "start")
-    pump(0, ZB, X0, Y0, X1, Y1, D0, D1)
-    own_ready(3)
-    pump(1, ZB, X0, Y0, X1, Y1, D0, D1)
-    own_ready(4)
-    acts[2].start()
-    whole(0)
-    seg = d // RING
-    hid = w2.shape[1]
-    for q in range(RING):
-        tile = fs[16 * q : 16 * q + 16].astype(F32)
-        vec_o[0:8, seg * q : seg * q + seg] = tile[0:8, 0:seg]
-        b1_o[0:1, hid * q : hid * q + hid] = tile[6:7, 0:hid]
-    own_x.wait()
+    FIRST = (ZB, X0, Y0)
+    THEN = (X1, Y1)
+    LAST = (D0, D1)
+
+    def assemble():
+        whole(SM)
+        seg = d // RING
+        hid = w2.shape[1]
+        for q in range(RING):
+            tile = fs[16 * q : 16 * q + 16].astype(F32)
+            vec_o[0:8, seg * q : seg * q + seg] = tile[0:8, 0:seg]
+            b1_o[0:1, hid * q : hid * q + hid] = tile[6:7, 0:hid]
 
     def first_norm(grp):
         def body(rows):
@@ -313,48 +334,27 @@
 
         chunks(n, 128, body)
 
-    first_norm(0)
-    whole(1)
-    save(fq, wq_o)
-    qkv[0:n] = dot(ac[0:n], fq[...], 1, 0).astype(BF)
-    acts[1].wait_recv()
-    fill_distance(dist.at[1], lays.at[1])
-    acts[0].wait_recv()
-    first_norm(1)
-    qkv[n : 2 * n] = dot(ac[n : 2 * n], fq[...], 1, 0).astype(BF)
-    save(qkv, qkv_o)
-    save(xb.at[1], x_o)
-    save(lays.at[1], lay_o)
+    def project(grp, side):
+        cols = pl.ds(side * half, half)
+        qkv[grp * n : grp * n + n, cols] = dot(ac[grp * n : grp * n + n], fq[:, cols], 1, 0).astype(BF)
+
     pairs = HEADS // 2
-    early = {
-        0: [(2, ZB, X0, Y0)],
-        1: [(2, X1, Y1)],
-        2: [(2, D0, D1)],
-        3: [(3, ZB, X0, Y0)],
-        5: [(3, X1, Y1)],
-        7: [(3, D0, D1)],
-        9: [(4, X0, Y0)],
-        10: [(4, ZB)],
-    }
-
-    @pl.loop(0, 2 * pairs)
-    def _(i):
-        grp, j = i // pairs, lax.rem(i, pairs)
-        rows = pl.ds(pl.multiple_of(grp * n, n), n)
-        attend_pair(qkv, rows, dist[grp], j, prob, 2 * i, ob, d)
-        pltpu.make_async_copy(
-            prob.at[pl.ds(2 * i, 2)], p_o.at[pl.ds(2 * i, 2)], ps.at[2 + i]
-        ).start()
-        for at, steps in early.items():
-
-            @pl.when(i == at)
-            def _(steps=steps):
-                for step in steps:
-                    pump(*step)
-
-    save(ob, o_o)
-    whole(2)
-    save(fp, wp_o)
+
+    def attention(start, stop, early):
+        @pl.loop(start, stop)
+        def _(i):
+            grp, j = i // pairs, lax.rem(i, pairs)
+            rows = pl.ds(pl.multiple_of(grp * n, n), n)
+            attend_pair(qkv, rows, dist[grp], j, prob, 2 * i, ob, d)
+            pltpu.make_async_copy(
+                prob.at[pl.ds(2 * i, 2)], p_o.at[pl.ds(2 * i, 2)], ps.at[2 + i]
+            ).start()
+            for at, steps in early.items():
+
+                @pl.when(i == at)
+                def _(steps=steps):
+                    for step in steps:
+                        pump(*step)
 
     def second_norm(rows):
         first = (
@@ -366,45 +366,108 @@
         nhat, _ = norm(first)
         ac[rows, :] = (nhat * vec_o[3:4] + vec_o[4:5]).astype(BF)
 
-    chunks(2 * n, 256, second_norm)
-    save(y1, y1_o)
-    save(ac, c_o)
-    pump(4, X1, Y1)
-    whole(3)
-    save(f1, w1_o)
-
     def hidden(cols):
         u = dot(ac[...], f1[:, cols], 1, 0) + b1_o[0:1, cols]
         phi = 0.5 + 0.5 * lax.erf(u * 0.7071067811865476)
         g[:, cols] = (u * phi).astype(BF)
         gs[:, cols] = (phi + u * (0.3989422804014327 * jnp.exp(-0.5 * u * u))).astype(BF)
 
-    chunks(g.shape[1], 256, hidden)
-    save(g, g_o)
-    save(gs, gs_o)
-    pump(4, D0, D1)
-    whole(4)
-    save(f2, w2_o)
+    def span(start, count, step, body):
+        chunks(count, step, lambda s: body(pl.ds(pl.multiple_of(start + s.start, step), step)))
 
     def result(rows):
         ac_rows = y1[rows, :] + dot(g[rows, :], f2[...], 1, 0) + vec_o[5:6]
         qkv[rows, 0:d] = ac_rows.astype(BF)
 
-    saves[1].wait()
+    for k in range(5):
+        hand_over(k, "start")
+    own_lay.wait()
+    fill_distance(dist.at[0], lays.at[0])
+    for k in range(4):
+        own_ready(k)
+    send_lay.start()
+    send_x.start()
+    pump(SM, *FIRST)
+    pump(QA, *FIRST)
+    pump(QB, *FIRST)
+    own_ready(4)
+    pump(SM, *THEN)
+    pump(QA, *THEN)
+    pump(QB, *THEN)
+    pump(SM, *LAST)
+    send_dog.start()
+    assemble()
+    own_x.wait()
+    first_norm(0)
+    pump(QA, *LAST)
+    pump(QB, *LAST)
+    pump(PR, *FIRST)
+    pump(UA, *FIRST)
+    whole(QA)
+    project(0, 0)
+    whole(QB)
+    project(0, 1)
+    attention(
+        0,
+        6,
+        {
+            0: [(PR, *THEN), (UB, *FIRST)],
+            2: [(UA, *THEN), (DA, *FIRST)],
+            5: [(PR, *LAST), (UB, *THEN), (DB, *FIRST)],
+        },
+    )
+    save(fq, wq_o)
+    send_lay.wait_recv()
+    fill_distance(dist.at[1], lays.at[1])
+    send_x.wait_recv()
+    first_norm(1)
+    project(1, 0)
+    project(1, 1)
+    qkv_saved = save(qkv, qkv_o)
+    save(xb.at[1], x_o)
+    save(lays.at[1], lay_o)
+    attention(
+        6,
+        12,
+        {
+            8: [(UA, *LAST), (DA, *THEN)],
+            10: [(UB, *LAST), (DB, *THEN)],
+        },
+    )
+    save(ob, o_o)
+    whole(PR)
+    save(fp, wp_o)
+    chunks(2 * n, 256, second_norm)
+    save(y1, y1_o)
+    save(ac, c_o)
+    pump(DA, *LAST)
+    whole(UA)
+    span(0, ff // 2, 256, hidden)
+    pump(DB, *LAST)
+    whole(UB)
+    save(f1, w1_o)
+    span(ff // 2, ff // 2, 256, hidden)
+    save(g, g_o)
+    save(gs, gs_o)
+    whole(DA)
+    whole(DB)
+    save(f2, w2_o)
+    qkv_saved.wait()
     chunks(2 * n, 512, result)
     save(qkv.at[:, pl.ds(0, d)], enc_o)
     for k in range(5):
         hand_over(k, "send")
-        gathers[k].finish()
-    acts[0].wait_send()
-    acts[1].wait_send()
-    acts[2].wait()
+    for piece in pieces:
+        piece.finish()
+    send_x.wait_send()
+    send_lay.wait_send()
+    send_dog.wait()
     for i in range(2 * pairs):
         pltpu.make_async_copy(
             prob.at[pl.ds(2 * i, 2)], p_o.at[pl.ds(2 * i, 2)], ps.at[2 + i]
         ).wait()
-    for k, copy in enumerate(saves):
-        if k != 1:
+    for copy in saves:
+        if copy is not qkv_saved:
             copy.wait()
 
 
@@ -460,8 +523,8 @@
             vmem((2 * n, ff), BF),
             dma((5, 2)),
             dma((5, 2)),
-            dma((5, 16)),
-            dma((5, 16)),
+            dma((8, 16)),
+            dma((8, 16)),
             dma((3,)),
             dma((3,)),
             dma((16,)),
@@ -603,9 +666,8 @@
     col = pl.multiple_of(j * 128, 128)
     eighth = jnp.asarray(0.125, BF)
     zero = jnp.zeros((), BF)
-    q = qkv[rows, pl.ds(col, 128)]
-    k = qkv[rows, pl.ds(d + col, 128)]
-    v = qkv[rows, pl.ds(2 * d + col, 128)]
+    cq, ck, cv = head_columns(j, d)
+    q, k, v = qkv[rows, cq], qkv[rows, ck], qkv[rows, cv]
     g = do[rows, pl.ds(col, 128)]
     both = g.astype(F32) * o[rows, pl.ds(col, 128)].astype(F32)
     dq = dk = dv = 0.0
@@ -619,9 +681,9 @@
         dk = dk + dot(ds, jnp.where(keep, q * eighth, zero), 1, 0)
         dv = dv + dot(p, gm, 1, 0)
         dq = dq + dot(jnp.where(keep, k * eighth, zero), ds, 0, 0)
-    qkv[rows, pl.ds(col, 128)] = dq.T.astype(BF)
-    qkv[rows, pl.ds(d + col, 128)] = dk.astype(BF)
-    qkv[rows, pl.ds(2 * d + col, 128)] = dv.astype(BF)
+    qkv[rows, cq] = dq.T.astype(BF)
+    qkv[rows, ck] = dk.astype(BF)
+    qkv[rows, cv] = dv.astype(BF)
 
 
 def backward_kernel(spread, *refs):
@@ -629,8 +691,8 @@
     (qkv_i, p_i, o_i, y1_i, c_i, g_i, gs_i, y_i) = refs[11:19]
     (oq, op, o1, o2, os_, enc_o, pg_o) = refs[19:26]
     (w2, w1, wp, qkv, g, du, c, ob, dz, y1, do, g2, gp, lays, sums) = refs[26:41]
-    got_sib, got, stages = refs[41:45], refs[45:49], refs[49:53]
-    (sgot, ss, rs, hs, hr, es, er, ts, tr, ls, ps) = refs[53:]
+    got_sib, got, stages = refs[41:48], refs[48:55], refs[55:59]
+    (sgot, ss, rs, hs, hr, es, er, ts, tr, ls, ps) = refs[59:]
     place = Place(spread)
     n, d = c.shape[0] // 2, c.shape[1]
     ff = w1.shape[1]
@@ -666,32 +728,63 @@
     acts[0].start()
     gq = du.at[pl.ds(0, d), pl.ds(0, wide)]
     g1 = g.at[pl.ds(0, d)]
+    DA, DB, UA, UB, PR, QA, QB = range(7)
+    cut = (
+        (3, 0, d // 2),
+        (3, d // 2, d // 2),
+        (2, 0, ff // 2),
+        (2, ff // 2, ff // 2),
+        (1, 0, d),
+        (0, 0, wide // 2),
+        (0, wide // 2, wide // 2),
+    )
     fulls = (gq, gp, g1, g2)
     outs = (oq, op, o1, o2)
-    rows_of = (48, 48, 48, ff // 16)
     sc = [
-        Scatter(place, fulls[k], rows_of[k], got_sib[k], got[k], ss.at[k], rs.at[k])
-        for k in range(4)
+        Scatter(
+            place,
+            fulls[w].at[:, pl.ds(at, size)],
+            fulls[w].shape[0] // 16,
+            got_sib[k],
+            got[k],
+            ss.at[k],
+            rs.at[k],
+        )
+        for k, (w, at, size) in enumerate(cut)
     ]
 
+    def back(k, go):
+        w, at, size = cut[k]
+        cols = pl.ds(at, size)
+        hand_back(place, stages[w].at[:, :, cols], outs[w].at[:, :, cols], hs.at[k], hr.at[k], go)
+
     def close(k):
-        total = sc[k].total()
-        half = rows_of[k] // 2
-        stages[k][0] = total[:half].astype(BF)
-        stages[k][1] = total[half:].astype(BF)
-        hand_back(place, stages[k], outs[k], hs.at[k], hr.at[k], "start")
-
-    QK, PR, W1, W2 = range(4)
+        w, at, size = cut[k]
+        total = sc[k].total().astype(BF)
+        half = total.shape[0] // 2
+        stages[w][0, :, at : at + size] = total[:half]
+        stages[w][1, :, at : at + size] = total[half:]
+        back(k, "start")
+
+    def do_steps(steps):
+        for what, k in steps:
+            if what == "c":
+                close(k)
+            else:
+                getattr(sc[k], {"b": "begin", "s": "second", "t": "third", "f": "fourth"}[what])()
+
     sums[...] = jnp.zeros_like(sums)
 
     def add_sum(row, v):
         sums[row : row + 1] += jnp.sum(v, axis=0, keepdims=True)
+
+    def span(start, count, step, body):
+        chunks(count, step, lambda s: body(pl.ds(pl.multiple_of(start + s.start, step), step)))
 
     for copy in (*lay_l, *dz_l):
         copy.wait()
     for grp in range(2):
         live = lays[grp].T[:, 3:4]
-
         for part in range(4):
             rows = pl.ds(grp * n + part * (n // 4), n // 4)
             keep = live[part * (n // 4) : (part + 1) * (n // 4)]
@@ -700,19 +793,11 @@
             add_sum(5, v)
     g_l.wait()
 
-    @pl.loop(0, 4)
-    def _(i):
-        z, other = lax.rem(i, 2), 1 - i // 2
-        start = (z * 2 + jnp.where(other == 1, 1 - place.c, place.c)) * (ff // 4)
-        cols = pl.ds(pl.multiple_of(start, 128), ff // 4)
-        g2[cols, :] = dot(g[:, cols], dz[...], 0, 0).astype(BF)
-
-        @pl.when(i == 1)
-        def _():
-            sc[W2].begin()
-
-    w2_l.wait()
-    du_l.wait()
+    def down_grad(at, size):
+        def body(rows):
+            g2[rows, pl.ds(at, size)] = dot(g[:, rows], dz[:, pl.ds(at, size)], 0, 0).astype(BF)
+
+        chunks(ff, 768, body)
 
     def hidden(cols):
         v = dot(dz[...], w2[cols, :], 1, 1) * du[:, cols].astype(F32)
@@ -721,12 +806,15 @@
         line = jnp.sum(r.astype(F32), axis=0, keepdims=True)
         sums[pl.ds(6 + cols.start // d, 1), pl.ds(pl.multiple_of(lax.rem(cols.start, d), 128), 256)] = line
 
-    chunks(ff, 256, hidden)
-    sc[W2].second()
     pairs = HEADS // 2
 
+    def turn(i):
+        third = i // 3
+        return 1 - lax.rem(third, 2), (third // 2) * 3 + lax.rem(i, 3)
+
     def fetch(i):
-        src = lax.rem(i + pairs, 2 * pairs) * 2
+        grp, j = turn(i)
+        src = (grp * pairs + j) * 2
         slot = lax.rem(i, 3)
         for half in range(2):
             yield pltpu.make_async_copy(
@@ -735,19 +823,8 @@
                 ps.at[slot, half],
             )
 
-    for i in range(3):
-        for copy in fetch(i):
-            copy.start()
-    c_l.wait()
-
     def up_grad(cols):
         g1[:, cols] = dot(c[...], du[:, cols], 0, 0).astype(BF)
-
-    chunks(ff, 768, up_grad)
-    sc[W1].begin()
-    sc[W2].third()
-    w1_l.wait()
-    y1_l.wait()
 
     def second_norm(rows):
         dc = dot(du[rows, :], w1[...], 1, 1)
@@ -760,45 +837,14 @@
         c[rows, :] = low
         add_sum(2, low.astype(F32))
 
-    def span(start, count, step, body):
-        chunks(count, step, lambda s: body(pl.ds(pl.multiple_of(start + s.start, step), step)))
-
-    span(0, n, 256, second_norm)
-    sc[W1].second()
-    span(n, n, 256, second_norm)
-    wq_l = load(wq_i, w1.at[:, pl.ds(0, wide)])
-    sc[W2].fourth()
-    o_l.wait()
-    wp_l.wait()
-    gp[...] = dot(ob[...], c[...], 0, 0).astype(BF)
-    sc[PR].begin()
-    do[...] = dot(c[...], wp[...], 1, 1).astype(BF)
-    x_l = (load(pat.at[place.m], c.at[pl.ds(0, n)]), load(x_i, c.at[pl.ds(n, n)]))
-    sc[W1].third()
-    for copy in x_l:
-        copy.wait()
-
     def first_norm(rows):
         nhat, _ = norm(c[rows, :].astype(F32))
         dz[rows, :] = (nhat * vec[0:1] + vec[1:2]).astype(BF)
 
-    chunks(2 * n, 256, first_norm)
-    qkv_l.wait()
-    work = {
-        0: lambda: sc[PR].second(),
-        1: lambda: close(W2),
-        3: lambda: sc[PR].third(),
-        4: lambda: sc[W1].fourth(),
-        7: lambda: sc[PR].fourth(),
-        8: lambda: close(W1),
-        10: lambda: close(PR),
-    }
-
-    def attention(start):
-        @pl.loop(start, start + pairs)
+    def attention(start, stop, work):
+        @pl.loop(start, stop)
         def _(i):
-            j = lax.rem(i, pairs)
-            grp = 1 - i // pairs
+            grp, j = turn(i)
             rows = pl.ds(pl.multiple_of(grp * n, n), n)
             for copy in fetch(i):
                 copy.wait()
@@ -814,12 +860,11 @@
                 for copy in fetch(i + 3):
                     copy.start()
 
-            for at, step in work.items():
-                if start <= at < start + pairs:
-
-                    @pl.when(i == at)
-                    def _(step=step):
-                        step()
+            for at, steps in work.items():
+
+                @pl.when(i == at)
+                def _(steps=steps):
+                    do_steps(steps)
 
     def input_grad(rows):
         da = dot(qkv[rows, :], w1[:, pl.ds(0, wide)], 1, 1)
@@ -828,46 +873,87 @@
         add_sum(1, da)
         c[rows, :] = (y1[rows, :] + unnorm(da, nhat, r, vec[0:1])).astype(BF)
 
-    attention(0)
+    def qkv_grad(side):
+        cols = pl.ds(side * (wide // 2), wide // 2)
+        gq[:, cols] = dot(dz[...], qkv[:, cols], 0, 0).astype(BF)
+
+    hops = (place.sib, place.xn, place.yn, place.zn)
+
+    def hop(i):
+        return rcopy(os_.at[place.m], sgot.at[i], ts.at[i], tr.at[i], hops[i])
+
+    def landed(i):
+        hop(i).wait()
+        os_[place.m] = os_[place.m] + sgot[i]
+
+    down_grad(0, d // 2)
+    do_steps([("b", DA)])
+    down_grad(d // 2, d // 2)
+    do_steps([("b", DB), ("s", DA)])
+    w2_l.wait()
+    du_l.wait()
+    chunks(ff, 256, hidden)
+    do_steps([("t", DA), ("s", DB)])
+    for i in range(3):
+        for copy in fetch(i):
+            copy.start()
+    c_l.wait()
+    span(0, ff // 2, 768, up_grad)
+    do_steps([("b", UA)])
+    span(ff // 2, ff // 2, 768, up_grad)
+    do_steps([("b", UB), ("f", DA), ("t", DB), ("s", UA)])
+    w1_l.wait()
+    y1_l.wait()
+    chunks(2 * n, 256, second_norm)
+    do_steps([("f", DB), ("t", UA), ("s", UB)])
+    wq_l = load(wq_i, w1.at[:, pl.ds(0, wide)])
+    o_l.wait()
+    wp_l.wait()
+    gp[...] = dot(ob[...], c[...], 0, 0).astype(BF)
+    do_steps([("b", PR)])
+    do[...] = dot(c[...], wp[...], 1, 1).astype(BF)
+    x_l = (load(pat.at[place.m], c.at[pl.ds(0, n)]), load(x_i, c.at[pl.ds(n, n)]))
+    for copy in x_l:
+        copy.wait()
+    chunks(2 * n, 256, first_norm)
+    qkv_l.wait()
+    attention(
+        0,
+        6,
+        {
+            2: [("c", DA), ("f", UA), ("t", UB), ("s", PR)],
+            5: [("c", DB), ("f", UB), ("t", PR)],
+        },
+    )
+    qkv_grad(0)
+    do_steps([("b", QA)])
+    attention(6, 9, {7: [("c", UA), ("f", PR), ("s", QA)]})
     wq_l.wait()
     span(n, n, 256, input_grad)
     acts[1].start()
-    attention(pairs)
-
-    def qkv_grad(cols):
-        gq[:, cols] = dot(dz[...], qkv[:, cols], 0, 0).astype(BF)
-
-    chunks(wide, 768, qkv_grad)
-    sc[QK].begin()
+    attention(9, 12, {9: [("c", UB), ("t", QA)], 11: [("c", PR)]})
+    qkv_grad(1)
+    do_steps([("b", QB)])
     span(0, n, 256, input_grad)
     pg_l = load(c.at[pl.ds(0, n)], pg_o.at[place.m])
     os_[place.m] = sums[...]
-    hops = (place.sib, place.xn, place.yn, place.zn)
-
-    def hop(i):
-        return rcopy(os_.at[place.m], sgot.at[i], ts.at[i], tr.at[i], hops[i])
-
-    def landed(i):
-        hop(i).wait()
-        os_[place.m] = os_[place.m] + sgot[i]
-
     hop(0).start()
-    sc[QK].second()
+    do_steps([("f", QA), ("s", QB)])
     landed(0)
     hop(1).start()
-    sc[QK].third()
+    do_steps([("t", QB)])
     landed(1)
     hop(2).start()
-    sc[QK].fourth()
+    do_steps([("c", QA), ("f", QB)])
     landed(2)
     hop(3).start()
-    close(QK)
+    do_steps([("c", QB)])
     landed(3)
     last = rcopy(os_.at[place.m], os_.at[place.m], ts.at[4], tr.at[4], place.pair)
     last.start()
-    for k in (W2, W1, PR, QK):
-        hand_back(place, stages[k], outs[k], hs.at[k], hr.at[k], "recv")
-        hand_back(place, stages[k], outs[k], hs.at[k], hr.at[k], "send")
+    for k in range(7):
+        back(k, "recv")
+        back(k, "send")
     last.wait_send()
     theirs = os_.at[1 - place.m]
     rcopy(theirs, theirs, ts.at[4], tr.at[4], place.pair).wait_recv()
@@ -882,6 +968,7 @@
     n, d = pat.shape[1:]
     wide, ff = kept[3].shape[1], kept[5].shape[1]
     shapes = ((48, wide), (48, d), (48, ff), (ff // 16, d))
+    cuts = 2 * ((ff // 16, d // 2),) + 2 * ((48, ff // 2),) + ((48, d),) + 2 * ((48, wide // 2),)
     sd = jax.ShapeDtypeStruct
     out = [sd((2, r // 2, k), BF) for r, k in shapes]
     out += [sd((2, 16, d), F32), sd((2, n, d), BF), sd((2, n, d), BF)]
@@ -909,15 +996,15 @@
             vmem((2,) + lay.shape, F32),
             vmem((16, d), F32),
         ]
-        + [vmem((2, 4 * r, k), BF) for r, k in shapes]
-        + [vmem((7, r, k), BF) for r, k in shapes]
+        + [vmem((2, 4 * r, k), BF) for r, k in cuts]
+        + [vmem((7, r, k), BF) for r, k in cuts]
         + [vmem((2, r // 2, k), BF) for r, k in shapes]
         + [
             vmem((4, 16, d), F32),
-            dma((4, 9)),
-            dma((4, 9)),
-            dma((4, 2)),
-            dma((4, 2)),
+            dma((7, 9)),
+            dma((7, 9)),
+            dma((7, 2)),
+            dma((7, 2)),
             dma((2,)),
             dma((2,)),
             dma((5,)),
@@ -962,6 +1049,7 @@
         spread, patches, out_grad, lay, pat2, dog2, lay2, fq, fp, f1, f2, vecs, *saved
     )
     pgrad = pgrad.astype(F32)
+    oq = oq.reshape(*oq.shape[:2], 2, 3, d // 2).swapaxes(2, 3).reshape(oq.shape)
     seg = d // RING
     vec = lax.dynamic_slice_in_dim(os_[:, :6], p * seg, seg, axis=2)
     hid = os_[:, 6 : 6 + w2.shape[1] * RING // d].reshape(2, -1)

time: 265 us -> 212 us (0.80)
  Pallas kernels: 248 us -> 194 us
    pallas_call x1, Pallas kernels: 135 us -> 105 us  [backward(): pl.pallas_call(functools.partial(backward_kernel, spread), out_shape=out,...]
    pallas_call x1, Pallas kernels: 113 us -> 89.4 us  [forward(): pl.pallas_call(functools.partial(forward_kernel, spread), out_shape=out,...]
where the time goes in v1:
time: 212 us
  Pallas kernels  194 us (92%)
  local copies, waits for them, and re-layouts  9.37 us (4%)
  other arithmetic  7.66 us (4%)
    pallas_call x1, Pallas kernels, backward(): pl.pallas_call(functools.partial(backward_kernel, spread), out_shape=out,...  105 us
    pallas_call x1, Pallas kernels, forward(): pl.pallas_call(functools.partial(forward_kernel, spread), out_shape=out,...  89.4 us
    another operation x15, local copies, waits for them, and re-layouts, small_pack(): jnp.stack([jnp.pad(v, ((0, 0), (0, 128 - v.shape[1]))) for v in (*parts,...  4.7 us

profile of v1, /device:TPU:0, one launch (start us, length us, event | category | flops | bytes accessed | tf_op | source)
XLA Modules:
  0.0 211.8 jit_solution(8217767108133285891)
XLA Ops:
  0.6 0.7 fusion.3
  1.3 0.1 fusion.2
  1.4 0.1 select_reduce_fusion.2
  1.6 0.4 fusion
  1.9 0.6 select_maximum_fusion.refs_2_
  2.6 0.7 pad_bitcast_fusion.6
  3.2 0.7 pad_bitcast_fusion.5
  3.9 0.7 pad_bitcast_fusion.4
  4.6 0.7 pad_bitcast_fusion.3
  5.2 0.7 pad_bitcast_fusion.2
  5.9 0.7 pad_bitcast_fusion.1
  6.6 0.7 pad_bitcast_fusion
  7.3 0.6 pad.39.refs_7_
  7.9 89.4 %forward.1 = (bf16[512,768]{1,0:T(8,128)(2,1)}, bf16[512,768]{1,0:T(8,128)(2,1)}, f32[8,512]{1,0:T(8,128)}, bf16[768,2304]{1,0:T(8,128)(2,1)}, bf16[768,768]{1,0...) custom-call(bf16[2,512,768]{2,1,0:T(8,128)(2,1)} %refs_0_.3, ...), custom_call_target="tpu_custom_call" | custom-call | tf_op jit(solution)/shard_map/forward/pallas_call | solution.py:500
  97.3 104.7 %backward.1 = (bf16[2,24,2304]{2,1,0:T(8,128)(2,1)}, bf16[2,24,768]{2,1,0:T(8,128)(2,1)}, bf16[2,24,3072]{2,1,0:T(8,128)(2,1)}, bf16[2,96,768]{2,1,0:T(8,128)(2,...) custom-call(bf16[2,512,768]{2,1,0:T(8,128)(2,1)} %refs_0_.3, ...), custom_call_target="tpu_custom_call" | custom-call | tf_op jit(solution)/shard_map/backward/pallas_call | solution.py:977
  201.9 0.0 copy-start.3
  201.9 0.0 copy-start.2
  202.0 0.0 copy-start.1
  202.0 3.4 %convert_element_type.89 = f32[2,512,768]{2,1,0:T(8,128)} convert(bf16[2,512,768]{2,1,0:T(8,128)(2,1)} %get-tuple-element.53) | non-fusion elementwise | flops 786432 | bytes 4718592 | tf_op jit(solution)/shard_map/convert_element_type | solution.py:1051
  205.4 0.0 copy-done.3
  205.4 0.2 reshape.179
  205.6 0.2 copy.50
  205.8 1.1 reshape.178
  206.9 0.0 copy-done.2
  206.9 0.9 convert_element_type.95
  207.8 0.0 copy-done.1
  207.8 0.9 convert_element_type.96
  208.7 0.0 copy-done.4
  208.7 0.7 convert_element_type.94
  209.3 0.7 constant_dynamic-slice_fusion.6
  210.0 0.6 constant_dynamic-slice_fusion.5
  210.7 1.1 copy.53
  (19 shorter events, 0.1 us)
Async XLA Ops:
  201.9 3.4 %copy-start.3 = (bf16[2,24,2304]{2,1,0:T(8,128)(2,1)S(1)}, bf16[2,24,2304]{2,1,0:T(8,128)(2,1)}, u32[]{:S(2)}) copy-start(bf16[2,24,2304]{2,1,0:T(8,128)(2,1)} %get-tuple-element.55) | copy-start | bytes 663556
  201.9 5.0 %copy-start.2 = (bf16[2,24,3072]{2,1,0:T(8,128)(2,1)S(1)}, bf16[2,24,3072]{2,1,0:T(8,128)(2,1)}, u32[]{:S(2)}) copy-start(bf16[2,24,3072]{2,1,0:T(8,128)(2,1)} %get-tuple-element.57) | copy-start | bytes 884740
  202.0 5.8 %copy-start.1 = (bf16[2,96,768]{2,1,0:T(8,128)(2,1)S(1)}, bf16[2,96,768]{2,1,0:T(8,128)(2,1)}, u32[]{:S(2)}) copy-start(bf16[2,96,768]{2,1,0:T(8,128)(2,1)} %get-tuple-element.58) | copy-start | bytes 884740
  205.3 3.3 %copy-start.4 = (bf16[2,24,768]{2,1,0:T(8,128)(2,1)S(1)}, bf16[2,24,768]{2,1,0:T(8,128)(2,1)}, u32[]{:S(2)}) copy-start(bf16[2,24,768]{2,1,0:T(8,128)(2,1)} %get-tuple-element.56) | copy-start | bytes 221188
  205.3 4.0 %copy-start.5 = (f32[2,16,768]{2,1,0:T(8,128)S(1)}, f32[2,16,768]{2,1,0:T(8,128)}, u32[]{:S(2)}) copy-start(f32[2,16,768]{2,1,0:T(8,128)} %get-tuple-element.54) | copy-start | bytes 294916
  205.3 5.3 %copy-start = (bf16[2,512,768]{2,1,0:T(8,128)(2,1)S(1)}, bf16[2,512,768]{2,1,0:T(8,128)(2,1)}, u32[]{:S(2)}) copy-start(bf16[2,512,768]{2,1,0:T(8,128)(2,1)} %get-tuple-element.89) | copy-start | bytes 4718596

commit v2 on v1

--- a/solution.py
+++ b/solution.py
@@ -18,32 +18,11 @@
 FAR = 1e33
 
 
-def packing(kind_ids, row_count):
-    slot_count = kind_ids.shape[0]
-    sides = jnp.where(kind_ids == 0, SIDE_S, jnp.where(kind_ids == 1, SIDE_M, SIDE_L)).astype(
-        jnp.int32
-    )
-    lengths = sides * sides
-    slots = jnp.arange(slot_count, dtype=jnp.int32)
-    ends = jnp.sum(jnp.where(slots[None, :] <= slots[:, None], lengths[None, :], 0), axis=1)
-    starts = ends - lengths
-    places = jnp.arange(row_count, dtype=jnp.int32)
-    inside = (
-        (ends <= row_count)[None, :]
-        & (places[:, None] >= starts[None, :])
-        & (places[:, None] < ends[None, :])
-    ).astype(jnp.int32)
-    filled = jnp.sum(inside, axis=1)
-    segment = jnp.sum(inside * slots[None, :], axis=1) + (1 - filled) * (slot_count + places)
-    offset = places - jnp.sum(inside * starts[None, :], axis=1)
-    side = jnp.sum(inside * sides[None, :], axis=1) + (1 - filled)
-    return segment, offset // side, offset % side, filled
-
-
 class Place:
     def __init__(self, spread):
         me = lax.axis_index("fsdp")
-        rest = lax.rem(me, spread)
+        self.rest = lax.rem(me, spread)
+        self.spread = spread
         p = me // spread
         self.p = p
         self.c = lax.rem(p, 2)
@@ -51,15 +30,15 @@
         self.y = lax.rem(p // 4, 2)
         self.m = lax.rem(p // 8, 2)
         self.z = lax.rem(p // 16, 2)
-        dev = lambda q: (q * spread + rest,)
-        sib = p + 1 - 2 * self.c
-        pair = p + 8 * (1 - 2 * self.m)
-        self.sib = dev(sib)
-        self.xn = dev(p + 2 * (1 - 2 * self.x))
-        self.yn = dev(p + 4 * (1 - 2 * self.y))
-        self.zn = dev(p + 16 * (1 - 2 * self.z))
-        self.pair = dev(pair)
-        self.cross = dev(pair + 1 - 2 * self.c)
+        self.sib = self.at(c=1 - self.c)
+        self.xn = self.at(x=1 - self.x)
+        self.yn = self.at(y=1 - self.y)
+        self.zn = self.at(z=1 - self.z)
+        self.pair = self.at(m=1 - self.m)
+
+    def at(self, **other):
+        z, m, y, x, c = (other.get(k, getattr(self, k)) for k in "zmyxc")
+        return ((((z * 2 + m) * 2 + y) * 2 + x) * 2 + c) * self.spread + self.rest,
 
     def chip(self, fz, fc, fy, fx):
         flip = lambda v, f: 1 - v if f else v
@@ -69,7 +48,17 @@
 
     def greet(self):
         barrier = pltpu.get_barrier_semaphore()
-        everyone = (self.sib, self.xn, self.yn, self.zn, self.pair, self.cross)
+        everyone = [self.sib, self.xn, self.yn]
+        for fz in range(2):
+            for fm in range(2):
+                for fc in range(2):
+                    if fz or fm:
+                        z, m, c = self.z, self.m, self.c
+                        everyone.append(
+                            self.at(
+                                z=1 - z if fz else z, m=1 - m if fm else m, c=1 - c if fc else c
+                            )
+                        )
         for other in everyone:
             pl.semaphore_signal(barrier, inc=1, device_id=other, device_id_type=MESH)
         pl.semaphore_wait(barrier, len(everyone))
@@ -99,15 +88,15 @@
         if way == "s":
             dev, slot = place.sib, 8 + kind
         else:
-            dev = {"x": place.xn, "y": place.yn, "z": place.zn}[way]
+            dev = {"x": place.xn, "y": place.yn}[way]
             fz, fy, fx = FLIPS[kind]
-            flips = {"x": (fz, fy, 1 - fx), "y": (fz, 1 - fy, fx), "z": (1 - fz, fy, fx)}[way]
+            flips = {"x": (fz, fy, 1 - fx), "y": (fz, 1 - fy, fx)}[way]
             slot = FLIPS.index(flips)
         view = self.block(kind)
         return rcopy(view, view, self.ssem.at[slot], self.rsem.at[slot], dev)
 
     AFTER = {
-        OWN: "zxys",
+        OWN: "xys",
         ZB: "xys",
         X0: "ys",
         X1: "s",
@@ -132,35 +121,48 @@
                 self.send(kind, way).wait_send()
 
 
-def hand_in(place, shard, spot, c_rows, ssem, rsem, go):
-    mine, theirs = shard.at[place.m], shard.at[1 - place.m]
-    here = lambda: pltpu.make_async_copy(mine, spot(place.c), rsem.at[place.c])
-    to_sib = lambda: rcopy(mine, spot(place.c), ssem.at[0], rsem.at[place.c], place.sib)
-    to_pair = lambda: rcopy(theirs, spot(place.c), ssem.at[1], rsem.at[place.c], place.pair)
-    to_cross = lambda: rcopy(theirs, spot(place.c), ssem.at[1], rsem.at[place.c], place.cross)
+def hand_in(place, shard, spot, ssem, rsem, go):
+    def legs():
+        for far in range(2):
+            for fm in range(2):
+                z = 1 - place.z if far else place.z
+                m = 1 - place.m if fm else place.m
+                yield far, fm, m, place.at(z=z, m=m, c=place.m)
+
+    def copy(far, fm, m, dev):
+        return rcopy(
+            shard.at[m], spot(far, None), ssem.at[2 * far + fm], rsem.at[2 * far + place.c], dev
+        )
+
+    here = place.c == place.m
     if go == "start":
-
-        @pl.when(place.c == place.m)
-        def _():
-            here().start()
-            to_pair().start()
-
-        @pl.when(place.c != place.m)
-        def _():
-            to_sib().start()
-            to_cross().start()
-
-    elif go == "recv":
+        for far, fm, m, dev in legs():
+            if far or fm:
+                copy(far, fm, m, dev).start()
+            else:
+
+                @pl.when(here)
+                def _():
+                    pltpu.make_async_copy(shard.at[m], spot(0, None), rsem.at[place.c]).start()
+
+                @pl.when(jnp.logical_not(here))
+                def _():
+                    copy(far, fm, m, dev).start()
+
+    elif go in ("near", "far"):
+        far = int(go == "far")
         for piece in range(2):
-            dst = spot(piece)
-            rcopy(dst, dst, ssem.at[1], rsem.at[piece], place.sib).wait_recv()
+            dst = spot(far, piece)
+            rcopy(dst, dst, ssem.at[0], rsem.at[2 * far + piece], place.sib).wait_recv()
     else:
-
-        @pl.when(place.c != place.m)
-        def _():
-            to_sib().wait_send()
-
-        to_pair().wait_send()
+        for far, fm, m, dev in legs():
+            if far or fm:
+                copy(far, fm, m, dev).wait_send()
+            else:
+
+                @pl.when(jnp.logical_not(here))
+                def _():
+                    copy(far, fm, m, dev).wait_send()
 
 
 def dot(a, b, ca, cb):
@@ -221,17 +223,48 @@
     o[rows, pl.ds(col, 128)] = total.T.astype(BF)
 
 
+def fill_layout(lay, kinds, n):
+    at = lax.broadcasted_iota(jnp.int32, (1, n), 1)
+    slots = kinds.shape[0]
+    segment, row, live = slots + at, at, jnp.zeros((1, n), jnp.int32)
+    col = jnp.zeros((1, n), jnp.int32)
+    start = jnp.int32(0)
+    for slot in range(slots):
+        kind = kinds[slot]
+        side = jnp.where(kind == 0, SIDE_S, jnp.where(kind == 1, SIDE_M, SIDE_L))
+        inverse = jnp.where(kind == 0, 1 / SIDE_S, jnp.where(kind == 1, 1 / SIDE_M, 1 / SIDE_L))
+        end = start + side * side
+        inside = (at >= start) & (at < end) & (end <= n)
+        offset = at - start
+        down = jnp.floor((offset.astype(F32) + 0.5) * inverse.astype(F32)).astype(jnp.int32)
+        segment = jnp.where(inside, slot, segment)
+        row = jnp.where(inside, down, row)
+        col = jnp.where(inside, offset - down * side, col)
+        live = jnp.where(inside, 1, live)
+        start = end
+    zero = jnp.zeros((4, n), F32)
+    lay[...] = jnp.concatenate([v.astype(F32) for v in (segment, row, col, live)] + [zero], axis=0)
+
+
 def forward_kernel(spread, *refs):
-    (pat, dog, lay, wq, wp, w1, w2, sm) = refs[:8]
-    (x_o, dog_o, lay_o, wq_o, wp_o, w1_o, w2_o, vec_o, b1_o) = refs[8:17]
-    (qkv_o, p_o, o_o, y1_o, c_o, g_o, gs_o, enc_o) = refs[17:25]
-    (fq, fp, f1, f2, fs, gq, gp, g1) = refs[25:33]
-    (lays, dist, xb, ac, qkv, prob, ob, y1, g, gs) = refs[33:43]
-    (hs, hr, ss, rs, as_, ar, ls, ps) = refs[43:]
+    (pat, dog, kinds, wq, wp, w1, w2) = refs[:7]
+    vectors = refs[7:14]
+    (x_o, dog_o, lay_o, wq_o, wp_o, w1_o, w2_o, vec_o, b1_o) = refs[14:23]
+    (qkv_o, p_o, o_o, y1_o, c_o, g_o, gs_o, enc_o) = refs[23:31]
+    (fq, fp, f1, f2, fs, gq, gp, g1) = refs[31:39]
+    (lays, dist, xb, ac, qkv, prob, ob, y1, g, gs, smf, sm) = refs[39:51]
+    (hs, hr, ss, rs, as_, ar, ls, ps) = refs[51:]
     place = Place(spread)
     d = xb.shape[2]
     n = xb.shape[1]
     ff = g.shape[1]
+    smf[...] = jnp.zeros_like(smf)
+    for at, ref in enumerate(vectors):
+        both = ref[...].astype(F32)
+        for m in range(2):
+            smf[m, at : at + 1, 0 : both.shape[1]] = both[m : m + 1]
+    for m in range(2):
+        sm[m] = smf[m].astype(BF)
     place.greet()
     hand = ((sm, fs, None, 16), (wq, fq, gq, 24), (wp, fp, gp, 24), (w1, f1, g1, 24))
     hand += ((w2, f2, None, w2.shape[1]),)
@@ -253,27 +286,26 @@
 
     def spot_of(k):
         _, full, stage, rows = hand[k]
-        if stage is not None:
-            return lambda piece: stage.at[piece]
-        own = place.chip(0, 0, 0, 0) * 2
-
-        def spot(piece):
-            place_of = place.p if piece is place.c else own + piece
-            return full.at[pl.ds(pl.multiple_of(place_of * rows, 16), rows)]
+
+        def spot(far, piece):
+            if stage is not None:
+                return stage.at[far, place.c if piece is None else piece]
+            at = place.p if piece is None else place.chip(far, 0, 0, 0) * 2 + piece
+            return full.at[pl.ds(pl.multiple_of(at * rows, 16), rows)]
 
         return spot
 
     def hand_over(k, go):
-        hand_in(place, hand[k][0], spot_of(k), hand[k][3], hs.at[k], hr.at[k], go)
-
-    def own_ready(k):
-        hand_over(k, "recv")
+        hand_in(place, hand[k][0], spot_of(k), hs.at[k], hr.at[k], go)
+
+    def ready(k, far):
+        hand_over(k, "far" if far else "near")
         _, full, stage, rows = hand[k]
         if stage is not None:
-            start = pl.multiple_of(place.chip(0, 0, 0, 0) * (2 * rows), 2 * rows)
+            start = pl.multiple_of(place.chip(far, 0, 0, 0) * (2 * rows), 2 * rows)
 
             def pack(src, dst):
-                both = [stage[piece, :, src].astype(F32) for piece in range(2)]
+                both = [stage[far, piece, :, src].astype(F32) for piece in range(2)]
                 full[pl.ds(start, 2 * rows), dst] = jnp.concatenate(both, axis=0).astype(BF)
 
             if k == 1:
@@ -287,7 +319,7 @@
                 pack(pl.ds(0, full.shape[1]), pl.ds(0, full.shape[1]))
         for i, (at, _) in enumerate(cut):
             if at == k:
-                pieces[i].start(OWN)
+                pieces[i].start(ZB if far else OWN)
 
     def pump(i, *kinds):
         for kind in kinds:
@@ -308,12 +340,10 @@
 
     send_x = rcopy(pat.at[1 - place.m], xb.at[1], as_.at[0], ar.at[0], place.pair)
     send_dog = rcopy(dog.at[1 - place.m], dog_o, as_.at[1], ar.at[1], place.pair)
-    send_lay = rcopy(lay, lays.at[1], as_.at[2], ar.at[2], place.pair)
+    send_lay = rcopy(lays.at[0], lays.at[1], as_.at[2], ar.at[2], place.pair)
     own_x = pltpu.make_async_copy(pat.at[place.m], xb.at[0], ps.at[0])
-    own_lay = pltpu.make_async_copy(lay, lays.at[0], ps.at[1])
-    own_lay.start()
     own_x.start()
-    FIRST = (ZB, X0, Y0)
+    FIRST = (X0, Y0)
     THEN = (X1, Y1)
     LAST = (D0, D1)
 
@@ -354,7 +384,10 @@
                 @pl.when(i == at)
                 def _(steps=steps):
                     for step in steps:
-                        pump(*step)
+                        if step[0] == "far":
+                            ready(step[1], 1)
+                        else:
+                            pump(*step)
 
     def second_norm(rows):
         first = (
@@ -381,41 +414,41 @@
 
     for k in range(5):
         hand_over(k, "start")
-    own_lay.wait()
-    fill_distance(dist.at[0], lays.at[0])
-    for k in range(4):
-        own_ready(k)
+    fill_layout(lays.at[0], kinds, n)
     send_lay.start()
     send_x.start()
+    fill_distance(dist.at[0], lays.at[0])
+    for k in range(3):
+        ready(k, 0)
+    ready(0, 1)
+    ready(1, 1)
+    ready(3, 0)
     pump(SM, *FIRST)
     pump(QA, *FIRST)
     pump(QB, *FIRST)
-    own_ready(4)
+    ready(4, 0)
     pump(SM, *THEN)
     pump(QA, *THEN)
     pump(QB, *THEN)
+    ready(2, 1)
+    pump(PR, *FIRST)
     pump(SM, *LAST)
-    send_dog.start()
     assemble()
     own_x.wait()
     first_norm(0)
     pump(QA, *LAST)
     pump(QB, *LAST)
-    pump(PR, *FIRST)
-    pump(UA, *FIRST)
+    send_dog.start()
     whole(QA)
     project(0, 0)
+    ready(3, 1)
+    pump(UA, *FIRST)
     whole(QB)
     project(0, 1)
-    attention(
-        0,
-        6,
-        {
-            0: [(PR, *THEN), (UB, *FIRST)],
-            2: [(UA, *THEN), (DA, *FIRST)],
-            5: [(PR, *LAST), (UB, *THEN), (DB, *FIRST)],
-        },
-    )
+    pump(UB, *FIRST)
+    pump(PR, *THEN)
+    attention(0, 1, {})
+    attention(1, 6, {1: [("far", 4)], 2: [(UA, *THEN)], 3: [(UB, *THEN)], 4: [(DA, *FIRST)], 5: [(DB, *FIRST), (PR, *LAST)]})
     save(fq, wq_o)
     send_lay.wait_recv()
     fill_distance(dist.at[1], lays.at[1])
@@ -425,15 +458,8 @@
     project(1, 1)
     qkv_saved = save(qkv, qkv_o)
     save(xb.at[1], x_o)
-    save(lays.at[1], lay_o)
-    attention(
-        6,
-        12,
-        {
-            8: [(UA, *LAST), (DA, *THEN)],
-            10: [(UB, *LAST), (DB, *THEN)],
-        },
-    )
+    save(lays, lay_o)
+    attention(6, 12, {7: [(DA, *THEN)], 8: [(UA, *LAST)], 9: [(DB, *THEN)], 10: [(UB, *LAST)]})
     save(ob, o_o)
     whole(PR)
     save(fp, wp_o)
@@ -471,7 +497,7 @@
             copy.wait()
 
 
-def forward(spread, pat, dog, lay, wq, wp, w1, w2, sm):
+def forward(spread, pat, dog, kinds, wq, wp, w1, w2, *vectors):
     any_, vm = pl.BlockSpec(memory_space=pl.ANY), pl.BlockSpec(memory_space=pltpu.VMEM)
     n, d = pat.shape[1:]
     ff = w2.shape[1] * RING
@@ -479,7 +505,7 @@
     out = [
         sd((n, d), BF),
         sd((n, d), BF),
-        sd(lay.shape, F32),
+        sd((2, 8, n), F32),
         sd((d, wq.shape[2]), BF),
         sd((d, d), BF),
         sd((d, ff), BF),
@@ -500,7 +526,7 @@
     return pl.pallas_call(
         functools.partial(forward_kernel, spread),
         out_shape=out,
-        in_specs=[any_] * 8,
+        in_specs=[any_] * 2 + [pl.BlockSpec(memory_space=pltpu.SMEM)] + [any_] * 4 + [vm] * 7,
         out_specs=[any_] * 7 + [vm] * 2 + [any_] * 8,
         scratch_shapes=[
             vmem((d, wq.shape[2]), BF),
@@ -508,10 +534,10 @@
             vmem((d, ff), BF),
             vmem((ff, d), BF),
             vmem((RING * 16, 128), BF),
-            vmem((2, 24, wq.shape[2]), BF),
-            vmem((2, 24, d), BF),
-            vmem((2, 24, ff), BF),
-            vmem((2,) + lay.shape, F32),
+            vmem((2, 2, 24, wq.shape[2]), BF),
+            vmem((2, 2, 24, d), BF),
+            vmem((2, 2, 24, ff), BF),
+            vmem((2, 8, n), F32),
             vmem((2, n, n), F32),
             vmem((2, n, d), BF),
             vmem((2 * n, d), BF),
@@ -521,8 +547,10 @@
             vmem((2 * n, d), F32),
             vmem((2 * n, ff), BF),
             vmem((2 * n, ff), BF),
-            dma((5, 2)),
-            dma((5, 2)),
+            vmem((2, 16, 128), F32),
+            vmem((2, 16, 128), BF),
+            dma((5, 4)),
+            dma((5, 4)),
             dma((8, 16)),
             dma((8, 16)),
             dma((3,)),
@@ -534,7 +562,7 @@
             collective_id=0, has_side_effects=True, vmem_limit_bytes=62 * 2**20
         ),
         name="forward",
-    )(pat, dog, lay, wq, wp, w1, w2, sm)
+    )(pat, dog, kinds, wq, wp, w1, w2, *vectors)
 
 
 class Scatter:
@@ -559,11 +587,11 @@
             self.pl.sib,
         )
 
-    MOVES = {D0: ("y", 0), D1: ("x", 1), X0: ("x", 2), X1: ("x", 3), Y0: ("y", 4), Y1: ("y", 5), ZB: ("z", 6)}
+    MOVES = {D0: ("y", 0), D1: ("x", 1), X0: ("x", 2), X1: ("x", 3), Y0: ("y", 4), Y1: ("y", 5)}
 
     def move(self, kind):
         way, slot = self.MOVES[kind]
-        dev = {"x": self.pl.xn, "y": self.pl.yn, "z": self.pl.zn}[way]
+        dev = {"x": self.pl.xn, "y": self.pl.yn}[way]
         return rcopy(
             self.full.at[pl.ds(self.start_of(kind), self.rows)],
             self.got.at[slot],
@@ -608,51 +636,54 @@
         self.add(Y1, (1,))
         self.move(Y1).start()
 
-    def fourth(self):
-        self.move(X1).wait()
-        self.move(Y1).wait()
-        self.add(ZB, (3, 5))
-        self.move(ZB).start()
-
-    def total(self):
-        self.move(X0).wait()
-        self.move(Y0).wait()
-        self.move(ZB).wait()
-        rows = pl.ds(self.start_of(OWN), self.rows)
+    def total(self, far):
+        kind, slots = (ZB, (X1, Y1)) if far else (OWN, (X0, Y0))
+        rows = pl.ds(self.start_of(kind), self.rows)
         total = self.full[rows, :].astype(F32)
-        for slot in (2, 4, 6):
-            total = total + self.got[slot].astype(F32)
-        return total
-
-
-def hand_back(place, stage, out, ssem, rsem, go):
-    if go == "start":
-
-        @pl.when(place.c == place.m)
-        def _():
-            pltpu.make_async_copy(stage.at[place.c], out.at[place.m], rsem.at[place.m]).start()
-            rcopy(
-                stage.at[1 - place.c], out.at[place.m], ssem.at[0], rsem.at[place.m], place.sib
-            ).start()
-
-        @pl.when(place.c != place.m)
-        def _():
-            rcopy(
-                stage.at[place.c], out.at[place.m], ssem.at[0], rsem.at[place.m], place.pair
-            ).start()
-            rcopy(
-                stage.at[1 - place.c], out.at[place.m], ssem.at[1], rsem.at[place.m], place.cross
-            ).start()
-
+        for move in slots:
+            self.move(move).wait()
+            total = total + self.got[self.MOVES[move][1]].astype(F32)
+        return total.astype(BF)
+
+
+def hand_back(place, stage, outs, ssem, rsem, go):
+    def leg(far, k):
+        z = 1 - place.z if far else place.z
+        return rcopy(
+            stage.at[far, k],
+            outs[far].at[place.m],
+            ssem.at[2 * far + k],
+            rsem.at[2 * far + place.m],
+            place.at(z=z, m=place.c, c=k),
+        )
+
+    def each(far, k, local, remote):
+        if far:
+            remote()
+        else:
+            here = jnp.logical_and(place.c == place.m, place.c == k)
+            pl.when(here)(local)
+            pl.when(jnp.logical_not(here))(remote)
+
+    if go in ("near", "far"):
+        far = int(go == "far")
+        for k in range(2):
+
+            def local(k=k):
+                pltpu.make_async_copy(
+                    stage.at[0, k], outs[0].at[place.m], rsem.at[place.m]
+                ).start()
+
+            each(far, k, local, lambda k=k: leg(far, k).start())
     elif go == "recv":
-        for k in range(2):
-            rcopy(out.at[k], out.at[k], ssem.at[0], rsem.at[k], place.sib).wait_recv()
+        for far in range(2):
+            for m in range(2):
+                dst = outs[far].at[m]
+                rcopy(dst, dst, ssem.at[0], rsem.at[2 * far + m], place.sib).wait_recv()
     else:
-        rcopy(stage.at[0], out.at[0], ssem.at[0], rsem.at[0], place.sib).wait_send()
-
-        @pl.when(place.c != place.m)
-        def _():
-            rcopy(stage.at[0], out.at[0], ssem.at[1], rsem.at[0], place.sib).wait_send()
+        for far in range(2):
+            for k in range(2):
+                each(far, k, lambda: None, lambda far=far, k=k: leg(far, k).wait_send())
 
 
 def unnorm(dn, nhat, r, gain):
@@ -687,12 +718,13 @@
 
 
 def backward_kernel(spread, *refs):
-    (pat, dog, lay, x_i, dog_i, lay_i, wq_i, wp_i, w1_i, w2_i, vec) = refs[:11]
-    (qkv_i, p_i, o_i, y1_i, c_i, g_i, gs_i, y_i) = refs[11:19]
-    (oq, op, o1, o2, os_, enc_o, pg_o) = refs[19:26]
-    (w2, w1, wp, qkv, g, du, c, ob, dz, y1, do, g2, gp, lays, sums) = refs[26:41]
-    got_sib, got, stages = refs[41:48], refs[48:55], refs[55:59]
-    (sgot, ss, rs, hs, hr, es, er, ts, tr, ls, ps) = refs[59:]
+    (pat, dog, x_i, dog_i, lay_i, wq_i, wp_i, w1_i, w2_i, vec) = refs[:10]
+    (qkv_i, p_i, o_i, y1_i, c_i, g_i, gs_i, y_i) = refs[10:18]
+    outs = (refs[18:22], refs[22:26])
+    (os_, enc_o, pg_o) = refs[26:29]
+    (w2, w1, wp, qkv, g, du, c, ob, dz, y1, do, g2, gp, lays, sums) = refs[29:44]
+    got_sib, got, stages = refs[44:51], refs[51:58], refs[58:62]
+    (sgot, ss, rs, hs, hr, es, er, ts, tr, ls, ps) = refs[62:]
     place = Place(spread)
     n, d = c.shape[0] // 2, c.shape[1]
     ff = w1.shape[1]
@@ -705,7 +737,7 @@
         loads.append(copy)
         return copy
 
-    lay_l = (load(lay, lays.at[0]), load(lay_i, lays.at[1]))
+    lay_l = (load(lay_i, lays),)
     dz_l = (
         load(dog.at[place.m], dz.at[pl.ds(0, n)]),
         load(dog_i, dz.at[pl.ds(n, n)]),
@@ -739,7 +771,6 @@
         (0, wide // 2, wide // 2),
     )
     fulls = (gq, gp, g1, g2)
-    outs = (oq, op, o1, o2)
     sc = [
         Scatter(
             place,
@@ -756,22 +787,23 @@
     def back(k, go):
         w, at, size = cut[k]
         cols = pl.ds(at, size)
-        hand_back(place, stages[w].at[:, :, cols], outs[w].at[:, :, cols], hs.at[k], hr.at[k], go)
-
-    def close(k):
+        into = [outs[far][w].at[:, :, cols] for far in range(2)]
+        hand_back(place, stages[w].at[:, :, :, cols], into, hs.at[k], hr.at[k], go)
+
+    def close(k, far):
         w, at, size = cut[k]
-        total = sc[k].total().astype(BF)
+        total = sc[k].total(far)
         half = total.shape[0] // 2
-        stages[w][0, :, at : at + size] = total[:half]
-        stages[w][1, :, at : at + size] = total[half:]
-        back(k, "start")
+        stages[w][far, 0, :, at : at + size] = total[:half]
+        stages[w][far, 1, :, at : at + size] = total[half:]
+        back(k, "far" if far else "near")
 
     def do_steps(steps):
         for what, k in steps:
-            if what == "c":
-                close(k)
+            if what in "fc":
+                close(k, int(what == "f"))
             else:
-                getattr(sc[k], {"b": "begin", "s": "second", "t": "third", "f": "fourth"}[what])()
+                getattr(sc[k], {"b": "begin", "s": "second", "t": "third"}[what])()
 
     sums[...] = jnp.zeros_like(sums)
 
@@ -963,22 +995,23 @@
     pg_l.wait()
 
 
-def backward(spread, pat, dog, lay, *kept):
+def backward(spread, pat, dog, *kept):
     any_, vm = pl.BlockSpec(memory_space=pl.ANY), pl.BlockSpec(memory_space=pltpu.VMEM)
     n, d = pat.shape[1:]
     wide, ff = kept[3].shape[1], kept[5].shape[1]
+    lay = kept[2]
     shapes = ((48, wide), (48, d), (48, ff), (ff // 16, d))
     cuts = 2 * ((ff // 16, d // 2),) + 2 * ((48, ff // 2),) + ((48, d),) + 2 * ((48, wide // 2),)
     sd = jax.ShapeDtypeStruct
-    out = [sd((2, r // 2, k), BF) for r, k in shapes]
+    out = 2 * [sd((2, r // 2, k), BF) for r, k in shapes]
     out += [sd((2, 16, d), F32), sd((2, n, d), BF), sd((2, n, d), BF)]
     dma = pltpu.SemaphoreType.DMA
     vmem = pltpu.VMEM
     return pl.pallas_call(
         functools.partial(backward_kernel, spread),
         out_shape=out,
-        in_specs=[any_] * 10 + [vm] + [any_] * 8,
-        out_specs=[any_] * 4 + [vm] + [any_] * 2,
+        in_specs=[any_] * 9 + [vm] + [any_] * 8,
+        out_specs=[any_] * 8 + [vm] + [any_] * 2,
         scratch_shapes=[
             vmem((ff, d), BF),
             vmem((d, ff), BF),
@@ -993,18 +1026,18 @@
             vmem((2 * n, d), BF),
             vmem((ff, d), BF),
             vmem((d, d), BF),
-            vmem((2,) + lay.shape, F32),
+            vmem(lay.shape, F32),
             vmem((16, d), F32),
         ]
         + [vmem((2, 4 * r, k), BF) for r, k in cuts]
-        + [vmem((7, r, k), BF) for r, k in cuts]
-        + [vmem((2, r // 2, k), BF) for r, k in shapes]
+        + [vmem((6, r, k), BF) for r, k in cuts]
+        + [vmem((2, 2, r // 2, k), BF) for r, k in shapes]
         + [
             vmem((4, 16, d), F32),
             dma((7, 9)),
             dma((7, 9)),
-            dma((7, 2)),
-            dma((7, 2)),
+            dma((7, 4)),
+            dma((7, 4)),
             dma((2,)),
             dma((2,)),
             dma((5,)),
@@ -1016,12 +1049,45 @@
             collective_id=1, has_side_effects=True, vmem_limit_bytes=62 * 2**20
         ),
         name="backward",
-    )(pat, dog, lay, *kept)
-
-
-def small_pack(parts, b1):
-    rows = jnp.stack([jnp.pad(v, ((0, 0), (0, 128 - v.shape[1]))) for v in (*parts, b1)], axis=1)
-    return jnp.pad(rows, ((0, 0), (0, 16 - rows.shape[1]), (0, 0)))
+    )(pat, dog, *kept)
+
+
+def finish_kernel(*refs):
+    (pg, enc), near, far = refs[:2], refs[2:6], refs[6:10]
+    (pg_o, enc_o), outs = refs[10:12], refs[12:16]
+    pg_o[...] = pg[...].astype(F32)
+    enc_o[...] = enc[...]
+
+    @pl.when(pl.program_id(0) == 0)
+    def _():
+        for k, out in enumerate(outs):
+            for m in range(2):
+                total = near[k][m].astype(F32) + far[k][m].astype(F32)
+                if k == 0:
+                    width = total.shape[1] // 6
+                    for at in range(6):
+                        part, side = at // 2, at % 2
+                        src = (side * 3 + part) * width
+                        out[m, :, at * width : (at + 1) * width] = total[:, src : src + width]
+                else:
+                    out[m] = total
+
+
+def finish(pg, enc, parts):
+    n, d = pg.shape[1:]
+    steps = 4
+    tile = pl.BlockSpec((2, n // steps, d), lambda i: (0, i, 0))
+    whole = [pl.BlockSpec(v.shape, lambda i: (0, 0, 0)) for v in parts]
+    sd = jax.ShapeDtypeStruct
+    return pl.pallas_call(
+        finish_kernel,
+        grid=(steps,),
+        out_shape=[sd(pg.shape, F32), sd(enc.shape, BF)] + [sd(v.shape, F32) for v in parts[:4]],
+        in_specs=[tile, tile] + whole,
+        out_specs=[tile, tile] + whole[:4],
+        compiler_params=pltpu.CompilerParams(vmem_limit_bytes=62 * 2**20),
+        name="finish",
+    )(pg, enc, *parts)
 
 
 def local(
@@ -1039,22 +1105,17 @@
         )
         wq, wp, w1, w2, b1 = ag(wq), ag(wp), ag(w1), ag(w2), ag(b1)
         parts = tuple(ag(v) for v in parts)
-    lay = jnp.stack([v.astype(F32) for v in packing(tile_kind, rows)])
-    lay = jnp.pad(lay, ((0, 4), (0, 0)))
-    sm = small_pack(parts, b1)
     pat2, dog2, lay2, fq, fp, f1, f2, vecs, _, *saved = forward(
-        spread, patches, out_grad, lay, wq, wp, w1, w2, sm
+        spread, patches, out_grad, tile_kind, wq, wp, w1, w2, *parts, b1
     )
-    oq, op, o1, o2, os_, encoded, pgrad = backward(
-        spread, patches, out_grad, lay, pat2, dog2, lay2, fq, fp, f1, f2, vecs, *saved
+    *shares, os_, encoded, pgrad = backward(
+        spread, patches, out_grad, pat2, dog2, lay2, fq, fp, f1, f2, vecs, *saved
     )
-    pgrad = pgrad.astype(F32)
-    oq = oq.reshape(*oq.shape[:2], 2, 3, d // 2).swapaxes(2, 3).reshape(oq.shape)
+    pgrad, encoded, *grads = finish(pgrad, encoded, shares)
     seg = d // RING
     vec = lax.dynamic_slice_in_dim(os_[:, :6], p * seg, seg, axis=2)
     hid = os_[:, 6 : 6 + w2.shape[1] * RING // d].reshape(2, -1)
     hid = lax.dynamic_slice_in_dim(hid, p * w2.shape[1], w2.shape[1], axis=1)
-    grads = [oq.astype(F32), op.astype(F32), o1.astype(F32), o2.astype(F32)]
     if spread > 1:
         rs = functools.partial(
             lax.psum_scatter, axis_name="fsdp", tiled=True, axis_index_groups=groups

time: 212 us -> 199 us (0.939)
  local copies, waits for them, and re-layouts: 9.37 us -> 1.34 us
  other arithmetic: 7.66 us -> 0 us
  Pallas kernels: 194 us -> 197 us
    convert_element_type x5 -> x0, other arithmetic: 6.13 us -> none  [the longest x1 3.38 us: local(): pgrad = pgrad.astype(F32)]
    pallas_call x0 -> x1, Pallas kernels: none -> 5.88 us  [finish(): pl.pallas_call(finish_kernel, grid=(steps,), out_shape=[sd(pg.shape, F32)...]
    another operation x15 -> x0, local copies, waits for them, and re-layouts: 4.7 us -> none  [small_pack(): jnp.stack([jnp.pad(v, ((0, 0), (0, 128 - v.shape[1]))) for v in (*parts,...]
    pallas_call x1, Pallas kernels: 105 us -> 101 us  [backward(): pl.pallas_call(functools.partial(backward_kernel, spread), out_shape=out,...]
where the time goes in v2:
time: 199 us
  Pallas kernels  197 us (99%)
    pallas_call x1, Pallas kernels, backward(): pl.pallas_call(functools.partial(backward_kernel, spread), out_shape=out,...  101 us
    pallas_call x1, Pallas kernels, forward(): pl.pallas_call(functools.partial(forward_kernel, spread), out_shape=out,...  90.1 us
    pallas_call x1, Pallas kernels, finish(): pl.pallas_call(finish_kernel, grid=(steps,), out_shape=[sd(pg.shape, F32)...  5.88 us

profile of v2, /device:TPU:0, one launch (start us, length us, event | category | flops | bytes accessed | tf_op | source)
XLA Modules:
  0.0 199.0 jit_solution(16750886826563423997)
XLA Ops:
  0.6 90.1 %forward.1 = (bf16[512,768]{1,0:T(8,128)(2,1)}, bf16[512,768]{1,0:T(8,128)(2,1)}, f32[2,8,512]{2,1,0:T(8,128)}, bf16[768,2304]{1,0:T(8,128)(2,1)}, bf16[768,768]...) custom-call(bf16[2,512,768]{2,1,0:T(8,128)(2,1)} %refs_0_.3, ...), custom_call_target="tpu_custom_call" | custom-call | tf_op jit(solution)/shard_map/forward/pallas_call | solution.py:526
  90.7 100.9 %backward.1 = (bf16[2,24,2304]{2,1,0:T(8,128)(2,1)}, bf16[2,24,768]{2,1,0:T(8,128)(2,1)}, bf16[2,24,3072]{2,1,0:T(8,128)(2,1)}, bf16[2,96,768]{2,1,0:T(8,128)(2,...) custom-call(bf16[2,512,768]{2,1,0:T(8,128)(2,1)} %refs_0_.3, ...), custom_call_target="tpu_custom_call" | custom-call | tf_op jit(solution)/shard_map/backward/pallas_call | solution.py:1010
  191.7 0.0 copy-start
  191.7 5.9 %finish.1 = (f32[2,512,768]{2,1,0:T(8,128)}, bf16[2,512,768]{2,1,0:T(8,128)(2,1)}, f32[2,24,2304]{2,1,0:T(8,128)}, f32[2,24,768]{2,1,0:T(8,128)}, f32[2,24,3072]{2,1,0:T(8,128)}, /*index=5*/f32[2,96,768]{2,1,0:T(8,128)}) custom-call(bf16[2,512,768]{2,1,0:T(8,128)(2,1)} %get-tuple-element.62.refs_0_, bf16[2,512,768]{2,1,0:T(8,128)(2,1)} %get-tuple-element.63.refs_1_, ...), custom_call_target="tpu_custom_call" | custom-call | tf_op jit(solution)/shard_map/finish/pallas_call | solution.py:1082
  197.6 0.0 copy-done
  197.6 0.7 constant_dynamic-slice_fusion.6
  198.3 0.6 constant_dynamic-slice_fusion.5
  (3 shorter events, 0.0 us)
Async XLA Ops:
  191.7 5.9 %copy-start = (f32[2,16,768]{2,1,0:T(8,128)S(1)}, f32[2,16,768]{2,1,0:T(8,128)}, u32[]{:S(2)}) copy-start(f32[2,16,768]{2,1,0:T(8,128)} %get-tuple-element.74) | copy-start | bytes 294916
